TPU v7x, 32 devices: a whole 2x2x4 slice. The times are simulated.
32 devices in a mesh: seq: 2 (over x), chan: 16 (over z, y, core).
Axes of the slice: x: 2, y: 2, z: 4, core: 2. Of those that a mesh axis runs over, the one named last changes fastest.
Arguments:
- activations: bfloat16 [1024, 4096], P('seq', 'chan'), may hold values from -6 to 6
- in_weight: bfloat16 [3, 4096, 4096], P(None, 'chan'), may hold values from -0.09375 to 0.09375
- short_taps: float32 [3, 3, 4096], P(None, None, 'chan'), may hold values from -3.5 to 3.5
- long_filter: bfloat16 [4096, 1024], P('chan', 'seq'), may hold values from -0.1875 to 0.1875
- skip_gain: float32 [4096], P('chan'), may hold values from -4 to 4
Outputs:
- mixed: bfloat16 [1024, 4096], P('seq', 'chan')
All inputs are finite; a program needn't handle non-finite values.
Results may differ from a plain program's by a relative error of at most 0.0076.
Values may be sent and summed in bfloat16 or wider, within the bound.
A program may use at most 64 MiB of HBM per device.

v0:
```python
import math

import jax
import jax.numpy as jnp
from jax import lax
from jax.sharding import PartitionSpec as P


def from_behind(block, axis, distance):
    devices = range(lax.axis_size(axis))
    route = [(i - distance, i) for i in devices if i - distance in devices]
    return lax.ppermute(block, axis, route)


def tables(length):
    double = 2 * length
    freq_index = jnp.arange(double, dtype=jnp.int32)
    phase = (freq_index[:, None] * freq_index[None, :] % double).astype(jnp.float32) * (
        2.0 * math.pi / double
    )
    return (jnp.cos(phase).astype(jnp.bfloat16), jnp.sin(phase).astype(jnp.bfloat16))


def spectrum(signal, cosine, sine):
    real_part = jnp.einsum("ft,...tc->...fc", cosine, signal, preferred_element_type=jnp.float32)
    imag_part = -jnp.einsum("ft,...tc->...fc", sine, signal, preferred_element_type=jnp.float32)
    return (real_part, imag_part)


def lag_spectrum(lags, cosine, sine):
    real_part = jnp.einsum("ft,...ct->...fc", cosine, lags, preferred_element_type=jnp.float32)
    imag_part = -jnp.einsum("ft,...ct->...fc", sine, lags, preferred_element_type=jnp.float32)
    return (real_part, imag_part)


def multiply_add(totals, filter_real, filter_imag, signal_real, signal_imag):
    return (
        totals[0] + filter_real * signal_real - filter_imag * signal_imag,
        totals[1] + filter_real * signal_imag + filter_imag * signal_real,
    )


def on_device(activations, in_weight, short_taps, long_filter, skip_gain):
    rows = activations.shape[0]
    channels = in_weight.shape[1]
    proj = jnp.einsum(
        "tk,sck->tsc",
        lax.all_gather(activations, "chan", axis=1, tiled=True),
        in_weight,
        preferred_element_type=jnp.float32,
    ).astype(jnp.bfloat16)
    earlier = from_behind(proj[rows - 2 :], "seq", 1)
    padded = jnp.concatenate([earlier, proj], axis=0).astype(jnp.float32)
    feat = (
        short_taps[:, 0, :] * padded[2:]
        + short_taps[:, 1, :] * padded[1:-1]
        + short_taps[:, 2, :] * padded[:-2]
    )
    gated = (feat[:, 1, :] * feat[:, 2, :]).astype(jnp.bfloat16)
    table_cos, table_sin = tables(rows)
    cosine = table_cos[:, :rows]
    sine = table_sin[:, :rows]
    double = 2 * rows
    seq_count = lax.axis_size("seq")
    all_lags = lax.all_gather(long_filter, "seq", axis=1, tiled=True)
    lag_blocks = jnp.transpose(all_lags.reshape(channels, seq_count, rows), (1, 0, 2))
    lag_real, lag_imag = lag_spectrum(lag_blocks, cosine, sine)
    spectra = jnp.stack([lag_real, lag_imag], axis=1)
    zero_spec = jnp.zeros((double, channels), jnp.float32)
    current = (zero_spec, zero_spec)
    previous = (zero_spec, zero_spec)
    moving = gated
    for section in range(seq_count):
        if section > 0:
            moving = from_behind(moving, "seq", 1)
        signal_real, signal_imag = spectrum(moving, cosine, sine)
        current = multiply_add(
            current, spectra[section, 0], spectra[section, 1], signal_real, signal_imag
        )
        if section > 0:
            previous = multiply_add(
                previous, spectra[section - 1, 0], spectra[section - 1, 1], signal_real, signal_imag
            )
    cur_real = current[0].astype(jnp.bfloat16)
    cur_imag = current[1].astype(jnp.bfloat16)
    prev_real = previous[0].astype(jnp.bfloat16)
    prev_imag = previous[1].astype(jnp.bfloat16)
    conv = (
        jnp.dot(table_cos[:rows], cur_real, preferred_element_type=jnp.float32)
        - jnp.dot(table_sin[:rows], cur_imag, preferred_element_type=jnp.float32)
        + jnp.dot(table_cos[rows:], prev_real, preferred_element_type=jnp.float32)
        - jnp.dot(table_sin[rows:], prev_imag, preferred_element_type=jnp.float32)
    ) / double
    return (feat[:, 0, :] * (conv + skip_gain * gated.astype(jnp.float32))).astype(jnp.bfloat16)


def solution(mesh):
    in_specs = (
        P("seq", "chan"),
        P(None, "chan", None),
        P(None, None, "chan"),
        P("chan", "seq"),
        P("chan"),
    )
    out_specs = P("seq", "chan")
    return jax.shard_map(
        on_device, mesh=mesh, in_specs=in_specs, out_specs=out_specs, check_vma=False
    )
```

profile of v0, /device:TPU:2, one launch (start us, length us, event | category | flops | bytes accessed | tf_op | source)
XLA Modules:
  0.0 98.1 jit_solution(17916444014881059678)
XLA Ops:
  6.5 0.0 copy-start.4
  6.5 0.0 all-gather.2.cloned.1.call-start
  6.5 0.7 all-gather.2.cloned.1.call-update
  7.3 1.1 %copy.6 = bf16[256,512]{0,1:T(8,128)(2,1)S(1)} copy(bf16[256,512]{1,0:T(8,128)(2,1)} %param.8) | data formatting | bytes 524288 | tf_op args[3]
  8.3 8.7 %all_gather.7 = bf16[256,1024]{0,1:T(8,128)(2,1)S(1)} all-gather(bf16[256,512]{0,1:T(8,128)(2,1)S(1)} %copy.6), channel_id=1, replica_groups=mesh['seq'=2,'chan'=16] {'seq'}, dimensions={1}, use_global_device_ids=true | all-gather | bytes 786432 | tf_op jit(solution)/shard_map/all_gather | solution.py:65
  17.1 0.2 copy.7
  17.3 0.0 copy-done.4
  17.3 15.7 %sine_convert_fusion = bf16[1024,1024]{1,0:T(8,128)(2,1)S(1)} fusion(), kind=kLoop, calls=%fused_computation.8 | loop fusion | flops 15728640 | bytes 2097152 | tf_op jit(solution)/shard_map/convert_element_type | solution.py:21
  33.0 0.0 copy-start
  33.0 2.1 %negate_bitcast_fusion = f32[2,1024,256]{2,1,0:T(8,128)} fusion(bf16[1024,1024]{1,0:T(8,128)(2,1)S(1)} %sine_convert_fusion, bf16[256,2,512]{2,0,1:T(8,128)(2,1)S(1)} %copy.7), kind=kOutput, calls=%fused_computation.13 | convolution fusion | flops 537395200 | bytes 3670016 | tf_op jit(solution)/shard_map/ft,...ct->...fc/dot_general | solution.py:32
  35.1 15.5 %cosine_convert_fusion = bf16[1024,1024]{1,0:T(8,128)(2,1)S(1)} fusion(), kind=kLoop, calls=%fused_computation.9 | loop fusion | flops 15728640 | bytes 2097152 | tf_op jit(solution)/shard_map/convert_element_type | solution.py:21
  50.7 0.0 copy-done
  50.7 2.1 %convolution_bitcast_fusion = f32[2,1024,256]{2,1,0:T(8,128)} fusion(bf16[1024,1024]{1,0:T(8,128)(2,1)S(1)} %cosine_convert_fusion, bf16[256,2,512]{2,0,1:T(8,128)(2,1)S(1)} %copy.7), kind=kOutput, calls=%fused_computation.14 | convolution fusion | flops 536870912 | bytes 3670016 | tf_op jit(solution)/shard_map/ft,...ct->...fc/dot_general | solution.py:31
  52.8 11.1 %all-gather.2.cloned.1.call-done = bf16[512,4096]{1,0:T(8,128)(2,1)} async-done(((bf16[512,256]{1,0:T(8,128)(2,1)}), bf16[512,4096]{1,0:T(8,128)(2,1)}) %all-gather.2.cloned.1.call-update) | async-done | bytes 4194320 | tf_op jit(solution)/shard_map/all_gather | solution.py:48
  63.9 7.5 %fusion.10 = bf16[512,3,256]{2,0,1:T(8,128)(2,1)S(1)} fusion(bf16[3,256,4096]{2,1,0:T(8,128)(2,1)} %param.6, bf16[512,4096]{1,0:T(8,128)(2,1)} %all-gather.2.cloned.1.call-done), kind=kOutput, calls=%fused_computation.20 | convolution fusion | flops 3221618688 | bytes 11272192 | tf_op jit(solution)/shard_map/tk,sck->tsc/dot_general | solution.py:46
  71.4 1.3 %collective-permute-start = (bf16[2,3,256]{2,0,1:T(2,128)(2,1)S(1)}, bf16[2,3,256]{2,0,1:T(2,128)(2,1)S(1)}, u32[]{:S(2)}, u32[]{:S(2)}) collective-permute-start(bf16[2,3,256]{2,0,1:T(2,128)(2,1)S(1)} %slice.94), channel_id=1, source_target_pairs={{0,16},{1,17},{2,18},{3,19},{4,20},{5,21},{6,22},{7,23},{8,24},{9,... | collective-permute-start | bytes 9224 | tf_op jit(solution)/shard_map/ppermute | solution.py:12
  72.8 4.2 %collective-permute-done = bf16[2,3,256]{2,0,1:T(2,128)(2,1)S(1)} collective-permute-done((bf16[2,3,256]{2,0,1:T(2,128)(2,1)S(1)}, bf16[2,3,256]{2,0,1:T(2,128)(2,1)S(1)}, u32[]{:S(2)}, u32[]{:S(2)}) %collective-permute-start) | collective-permute-done | bytes 3104 | tf_op jit(solution)/shard_map/ppermute | solution.py:12
  76.9 0.2 maximum_convert_fusion
  77.1 0.5 fusion.8
  77.6 0.0 copy-start.1
  77.6 0.1 fusion.35
  77.6 1.4 %collective-permute-start.1 = (bf16[512,256]{1,0:T(8,128)(2,1)S(1)}, bf16[512,256]{1,0:T(8,128)(2,1)S(1)}, u32[]{:S(2)}, u32[]{:S(2)}) collective-permute-start(bf16[512,256]{1,0:T(8,128)(2,1)S(1)} %fusion.35), channel_id=1, source_target_pairs={{0,16},{1,17},{2,18},{3,19},{4,20},{5,21},{6,22},{7,23},{8,24},{9,... | collective-permute-start | bytes 786440 | tf_op jit(solution)/shard_map/ppermute | solution.py:12
  79.1 0.4 fusion.29
  79.5 0.0 copy-done.1
  79.5 0.4 convolution_negate_fusion.1
  80.0 0.0 copy-start.2
  80.0 0.0 copy-start.3
  80.0 7.0 %collective-permute-done.1 = bf16[512,256]{1,0:T(8,128)(2,1)S(1)} collective-permute-done((bf16[512,256]{1,0:T(8,128)(2,1)S(1)}, bf16[512,256]{1,0:T(8,128)(2,1)S(1)}, u32[]{:S(2)}, u32[]{:S(2)}) %collective-permute-start.1) | collective-permute-done | bytes 262176 | tf_op jit(solution)/shard_map/ppermute | solution.py:12
  87.0 0.4 fusion.27
  87.4 0.4 convolution_negate_fusion
  87.9 0.0 copy-done.2
  87.9 0.0 copy-done.3
  87.9 0.7 fusion.20
  88.6 0.7 convolution_subtract_fusion.1
  89.4 0.0 copy-start.5
  89.4 0.5 convolution_add_fusion
  89.9 0.1 copy-done.5
  90.0 1.2 %fusion.16 = bf16[512,256]{1,0:T(8,128)(2,1)} fusion(f32[512,256]{1,0:T(8,128)S(1)} %convolution_add_fusion, bf16[1024,1024]{1,0:T(8,128)(2,1)S(1)} %copy-done.1, f32[1024,256]{1,0:T(8,128)S(1)} %fusion.27, f32[1024,256]{1,0:T(8,128)S(1)} %convolution_negate_fusion, f32[2,1024,256]{2,1,0:T(8,128)S(1)} %copy-done.3, f32[2,1024,256]{2,1,0:T(8,128)S(1)} %copy-done.2, ...), kind=kOutput, calls=%fused_computation.29 | convolution fusion | flops 270401536 | bytes 6816768 | tf_op jit(solution)/shard_map/dot_general | solution.py:92
  (4 shorter events, 0.0 us)
Async XLA Ops:
  6.5 10.8 %copy-start.4 = (f32[3,3,256]{2,1,0:T(4,128)S(1)}, f32[3,3,256]{2,1,0:T(4,128)}, u32[]{:S(2)}) copy-start(f32[3,3,256]{2,1,0:T(4,128)} %param.7) | copy-start | bytes 27652
  6.5 57.4 %all-gather.2.cloned.1.call-start = ((), (), s32[]{:S(2)}) async-start(), calls=%async_computation | async-start | bytes 4456448 | tf_op jit(solution)/shard_map/all_gather | solution.py:48
  33.0 17.7 %copy-start = (bf16[1024,1024]{1,0:T(8,128)(2,1)}, bf16[1024,1024]{1,0:T(8,128)(2,1)S(1)}, u32[]{:S(2)}) copy-start(bf16[1024,1024]{1,0:T(8,128)(2,1)S(1)} %sine_convert_fusion) | copy-start | bytes 6291460
  71.4 5.5 %collective-permute-start = (bf16[2,3,256]{2,0,1:T(2,128)(2,1)S(1)}, bf16[2,3,256]{2,0,1:T(2,128)(2,1)S(1)}, u32[]{:S(2)}, u32[]{:S(2)}) collective-permute-start(bf16[2,3,256]{2,0,1:T(2,128)(2,1)S(1)} %slice.94), channel_id=1, source_target_pairs={{0,16},{1,17},{2,18},{3,19},{4,20},{5,21},{6,22},{7,23},{8,24},{9,... | collective-permute-start | bytes 9224 | tf_op jit(solution)/shard_map/ppermute | solution.py:12
  77.6 1.9 %copy-start.1 = (bf16[1024,1024]{1,0:T(8,128)(2,1)S(1)}, bf16[1024,1024]{1,0:T(8,128)(2,1)}, u32[]{:S(2)}) copy-start(bf16[1024,1024]{1,0:T(8,128)(2,1)} %copy-done) | copy-start | bytes 6291460
  77.6 9.4 %collective-permute-start.1 = (bf16[512,256]{1,0:T(8,128)(2,1)S(1)}, bf16[512,256]{1,0:T(8,128)(2,1)S(1)}, u32[]{:S(2)}, u32[]{:S(2)}) collective-permute-start(bf16[512,256]{1,0:T(8,128)(2,1)S(1)} %fusion.35), channel_id=1, source_target_pairs={{0,16},{1,17},{2,18},{3,19},{4,20},{5,21},{6,22},{7,23},{8,24},{9,... | collective-permute-start | bytes 786440 | tf_op jit(solution)/shard_map/ppermute | solution.py:12
  80.0 7.9 %copy-start.2 = (f32[2,1024,256]{2,1,0:T(8,128)S(1)}, f32[2,1024,256]{2,1,0:T(8,128)}, u32[]{:S(2)}) copy-start(f32[2,1024,256]{2,1,0:T(8,128)} %negate_bitcast_fusion) | copy-start | bytes 6291460
  80.0 7.9 %copy-start.3 = (f32[2,1024,256]{2,1,0:T(8,128)S(1)}, f32[2,1024,256]{2,1,0:T(8,128)}, u32[]{:S(2)}) copy-start(f32[2,1024,256]{2,1,0:T(8,128)} %convolution_bitcast_fusion) | copy-start | bytes 6291460
  89.4 0.7 copy-start.5
Sparse Core Ops, SparseCore 0:
  9.5 54.3 all-gather.1
where the time goes:
time: 98.8 us; the launch traced here: 98.1 us
  other arithmetic  31.9 us (32%)
  waiting for transfers between devices  23 us (23%)
  matrix products  16.7 us (17%)
  between operations  13.6 us (14%)
  blocking collectives  8.72 us (9%)
  starting transfers between devices  2.72 us (3%)
  local copies, waits for them, and re-layouts  1.47 us (1%)
    convert_element_type x1, other arithmetic, tables(): jnp.sin(phase).astype(jnp.bfloat16)  15.7 us
    convert_element_type x1, other arithmetic, tables(): jnp.cos(phase).astype(jnp.bfloat16)  15.5 us
    ppermute x2, waiting for transfers between devices, from_behind(): return lax.ppermute(block, axis, route)  11.2 us
    all_gather x1, waiting for transfers between devices, on_device(): lax.all_gather(activations, 'chan', axis=1, tiled=True)  11.1 us
    all_gather x1, blocking collectives, on_device(): all_lags = lax.all_gather(long_filter, 'seq', axis=1, tiled=True)  8.72 us
    dot_general x1, matrix products, on_device(): jnp.einsum('tk,sck->tsc', lax.all_gather(activations, 'chan', axis=1, til...  7.51 us
    ppermute x2, starting transfers between devices, from_behind(): return lax.ppermute(block, axis, route)  2.72 us
    dot_general x1, matrix products, lag_spectrum(): jnp.einsum('ft,...ct->...fc', sine, lags, preferred_element_type=jnp.floa...  2.12 us
  transfers between devices with their start and end apart: 3, of which 3 were waited for; matrix products, arithmetic and copies ran while one was open for 38% of the time, Pallas kernels for 0%

commit v1 on v0

v1 whole, which is shorter than its diff:
```python
import functools
import math

import jax
import jax.numpy as jnp
import ml_dtypes
import numpy as np
from jax import lax
from jax.experimental import pallas as pl
from jax.experimental.pallas import tpu as pltpu
from jax.sharding import PartitionSpec as P

MESH = pl.DeviceIdType.MESH
F32 = jnp.float32
BF16 = jnp.bfloat16
CHUNKS = 4
HALO = 8


def from_behind(block, axis, distance):
    devices = range(lax.axis_size(axis))
    route = [(i - distance, i) for i in devices if i - distance in devices]
    return lax.ppermute(block, axis, route)


def half_tables(length):
    double = 2 * length
    index = np.arange(length, dtype=np.int64)
    phase = ((index[:, None] * index[None, :]) % double).astype(np.float32) * np.float32(
        2.0 * math.pi / double
    )
    cosine = np.cos(phase)
    sine = -np.sin(phase)
    sine[0] = 1.0 - 2.0 * (index % 2)
    forward = np.concatenate([cosine, sine], axis=0).astype(ml_dtypes.bfloat16)
    inverse = np.concatenate([cosine, sine.T], axis=1).astype(ml_dtypes.bfloat16)
    return forward, inverse


def times(fil_real, fil_imag, sig_real, sig_imag, first):
    cross = jnp.where(first, 0.0, fil_imag)
    real_part = fil_real * sig_real - cross * sig_imag
    imag_part = jnp.where(first, fil_imag, fil_real) * sig_imag + cross * sig_real
    return real_part, imag_part


def nt_dot(a, b):
    return lax.dot_general(a, b, (((1,), (1,)), ((), ())), preferred_element_type=F32)


def fused_kernel(
    chips, act, weight, taps, filt, gain, fwd_in, inv_in, out,
    blocks, wv, acc, proj, gated, gated_in, lags, fwd, inv, spec, total,
    ring_send, ring_recv, core_send, core_recv, own_sem, weight_sem, load_sem,
    seq_send, seq_recv,
):
    rows, depth = act.shape
    width = taps.shape[-1]
    size = rows // CHUNKS
    far = chips // 2
    full = far - 1
    last_slot = 2 * full + 1

    seq = lax.axis_index("seq")
    chan = lax.axis_index("chan")
    chip, core = chan // 2, chan % 2

    def chip_at(place):
        place = lax.rem(place + 2 * chips, chips)
        return jnp.where(place < far, 2 * place, 2 * (chips - 1 - place) + 1)

    place = jnp.where(chip % 2 == 0, chip // 2, chips - 1 - chip // 2)
    ahead = (chip_at(place + 1) * 2 + core, chip_at(place - 1) * 2 + core)
    sibling = chip * 2 + 1 - core

    def slot_of(d, hop):
        if hop == 0:
            return 0
        return last_slot if hop == far else 1 + d * full + hop - 1

    def slots_at(hop):
        return [slot_of(0, hop)] if hop in (0, far) else [slot_of(0, hop), slot_of(1, hop)]

    def chunk(t):
        return pl.ds(pl.multiple_of(t * size, size), size)

    def ring_copy(d, hop, t):
        src = act.at[chunk(t)] if hop == 1 else blocks.at[0, slot_of(d, hop - 1), t]
        slot = slot_of(d, hop)
        return pltpu.make_async_remote_copy(
            src_ref=src, dst_ref=blocks.at[0, slot, t],
            send_sem=ring_send.at[slot, t], recv_sem=ring_recv.at[slot, t],
            device_id=(seq, ahead[d]), device_id_type=MESH,
        )

    def core_copy(slot, t):
        src = act.at[chunk(t)] if slot == 0 else blocks.at[0, slot, t]
        return pltpu.make_async_remote_copy(
            src_ref=src, dst_ref=blocks.at[1, slot, t],
            send_sem=core_send.at[slot, t], recv_sem=core_recv.at[slot, t],
            device_id=(seq, sibling), device_id_type=MESH,
        )

    def seq_copy(src, dst, n):
        return pltpu.make_async_remote_copy(
            src_ref=src, dst_ref=dst, send_sem=seq_send.at[n], recv_sem=seq_recv.at[n],
            device_id=(1 - seq, chan), device_id_type=MESH,
        )

    def gated_copy(t):
        return seq_copy(gated.at[chunk(t)], gated_in.at[chunk(t)], t)

    def halo_copy():
        return seq_copy(proj.at[:, pl.ds(rows, HALO)], proj.at[:, pl.ds(0, HALO)], CHUNKS)

    def filter_copy():
        return seq_copy(filt, lags.at[0], CHUNKS + 1)

    def own_copy(t):
        return pltpu.make_async_copy(act.at[chunk(t)], blocks.at[0, 0, t], own_sem.at[t])

    def weight_copy(side, slot):
        if slot == 0:
            origin = chip
        elif slot == last_slot:
            origin = chip_at(place + far)
        elif slot <= full:
            origin = chip_at(place - slot)
        else:
            origin = chip_at(place + slot - full)
        block = origin * 2 + (core if side == 0 else 1 - core)
        cols = pl.ds(pl.multiple_of(block * depth, depth), depth)
        return pltpu.make_async_copy(
            weight.at[:, :, cols], wv.at[side, slot], weight_sem.at[side, slot]
        )

    fwd_copy = pltpu.make_async_copy(fwd_in, fwd, load_sem.at[0])
    inv_copy = pltpu.make_async_copy(inv_in, inv, load_sem.at[1])
    lag_copy = pltpu.make_async_copy(filt, lags.at[seq], load_sem.at[2])

    for t in range(CHUNKS):
        own_copy(t).start()
    for slot in range(last_slot + 1):
        for side in range(2):
            weight_copy(side, slot).start()
    lag_copy.start()
    fwd_copy.start()
    inv_copy.start()

    barrier = pltpu.get_barrier_semaphore()
    for target in ((seq, ahead[0]), (seq, ahead[1]), (seq, sibling), (1 - seq, chan)):
        pl.semaphore_signal(barrier, inc=1, device_id=target, device_id_type=MESH)
    pl.semaphore_wait(barrier, 4)

    @pl.when(seq == 0)
    def _():
        proj[:, pl.ds(0, HALO), :] = jnp.zeros((3, HALO, width), F32)

    def short(stream, t):
        window = proj[stream, pl.ds(pl.multiple_of(t * size, size), size + HALO), :]
        return (
            taps[stream, 0, :][None] * window[HALO:]
            + taps[stream, 1, :][None] * window[HALO - 1 : HALO - 1 + size]
            + taps[stream, 2, :][None] * window[HALO - 2 : HALO - 2 + size]
        )

    def gate(t):
        gated[chunk(t), :] = (short(1, t) * short(2, t)).astype(BF16)

    def product(side, hop, t):
        slots = slots_at(hop)

        @pl.when(t == 0)
        def _():
            for slot in slots:
                weight_copy(side, slot).wait()

        x = jnp.concatenate([blocks[side, slot, t] for slot in slots], axis=1)
        w = jnp.concatenate(
            [wv[side, slot].reshape(3 * width, depth) for slot in slots], axis=1
        )
        return nt_dot(x, w)

    hops = list(range(far, -1, -1))

    def step(g, carry):
        for hop in hops:
            t = g - hop

            @pl.when((t >= 0) & (t < CHUNKS))
            def _(hop=hop, t=t):
                if hop == 0:
                    for d in range(2):
                        ring_copy(d, 1, t).start()
                    core_copy(0, t).start()
                elif hop < far:
                    for d in range(2):
                        ring_copy(d, hop, t).wait_recv()
                        if hop < full:
                            ring_copy(d, hop + 1, t).start()
                        else:

                            @pl.when(t % 2 == d)
                            def _(d=d):
                                ring_copy(d, far, t).start()

                        core_copy(slot_of(d, hop), t).start()
                else:
                    ring_copy(0, far, t).wait_recv()
                    core_copy(last_slot, t).start()

        @pl.when((g == 0) & (seq == 0))
        def _():
            filter_copy().start()

        for side in range(2):
            for hop in hops:
                t = g - hop

                @pl.when((t >= 0) & (t < CHUNKS))
                def _(side=side, hop=hop, t=t):
                    if side == 1:
                        for slot in slots_at(hop):
                            core_copy(slot, t).wait_recv()
                    if side == 0 and hop == 0:
                        own_copy(t).wait()
                        acc[t] = product(side, hop, t)
                    else:
                        acc[t] += product(side, hop, t)

        @pl.when(g == full)
        def _():
            fwd_copy.wait()
            inv_copy.wait()
            lag_copy.wait()

            @pl.when(seq == 1)
            def _():
                filter_copy().wait_recv()

            spec[0] = nt_dot(fwd[...], lags[0])

            @pl.when(seq == 1)
            def _():
                sign = 1.0 - 2.0 * (
                    lax.broadcasted_iota(jnp.int32, (2 * rows, width), 0) % 2
                ).astype(F32)
                spec[1] = nt_dot(fwd[...], lags[1]) + sign * spec[0]

        done = g - far

        @pl.when(done >= 0)
        def _():
            for stream in range(3):
                cols = slice(stream * width, (stream + 1) * width)
                proj[stream, pl.ds(pl.multiple_of(done * size + HALO, HALO), size), :] = (
                    acc[done, :, cols].astype(BF16).astype(F32)
                )

            @pl.when((seq == 0) & (done == CHUNKS - 1))
            def _():
                halo_copy().start()

            @pl.when((seq == 0) | (done > 0))
            def _():
                gate(done)

            @pl.when(seq == 0)
            def _():
                gated_copy(done).start()

        return carry

    lax.fori_loop(0, CHUNKS + far, step, 0)

    @pl.when(seq == 1)
    def _():
        halo_copy().wait_recv()
        gate(0)

    first = lax.broadcasted_iota(jnp.int32, (rows, width), 0) == 0

    def term(lag, source):
        signal = jnp.dot(fwd[...], source[...], preferred_element_type=F32)
        return times(
            spec[lag, :rows], spec[lag, rows:], signal[:rows], signal[rows:], first
        )

    total[0], total[1] = term(0, gated)

    @pl.when(seq == 1)
    def _():
        for t in range(CHUNKS):
            gated_copy(t).wait_recv()
        real_part, imag_part = term(1, gated_in)
        total[0] += real_part
        total[1] += imag_part

    scale = jnp.where(first, 0.5, 1.0) / rows
    spectrum = jnp.concatenate(
        [(total[0] * scale).astype(BF16), (total[1] * scale).astype(BF16)], axis=0
    )
    conv = jnp.dot(inv[...], spectrum, preferred_element_type=F32)
    for t in range(CHUNKS):
        here = slice(t * size, (t + 1) * size)
        out[here, :] = (
            short(0, t) * (conv[here] + gain[...] * gated[here, :].astype(F32))
        ).astype(BF16)

    def finish(t, carry):
        for hop in range(1, far):
            for d in range(2):
                ring_copy(d, hop, t).wait_send()
        for d in range(2):

            @pl.when(t % 2 == d)
            def _(d=d):
                ring_copy(d, far, t).wait_send()

        for slot in range(last_slot + 1):
            core_copy(slot, t).wait_send()

        @pl.when(seq == 0)
        def _():
            gated_copy(t).wait_send()

        return carry

    lax.fori_loop(0, CHUNKS, finish, 0)

    @pl.when(seq == 0)
    def _():
        halo_copy().wait_send()
        filter_copy().wait_send()


def fused(chips, activations, in_weight, short_taps, long_filter, skip_gain):
    rows, depth = activations.shape
    width = in_weight.shape[1]
    forward, inverse = half_tables(rows)
    size = rows // CHUNKS
    here = pl.BlockSpec(memory_space=pltpu.VMEM)
    there = pl.BlockSpec(memory_space=pl.ANY)
    dma = pltpu.SemaphoreType.DMA
    return pl.pallas_call(
        functools.partial(fused_kernel, chips),
        out_shape=jax.ShapeDtypeStruct((rows, width), BF16),
        in_specs=[there, there, here, there, here, there, there],
        out_specs=here,
        scratch_shapes=[
            pltpu.VMEM((2, chips, CHUNKS, size, depth), BF16),
            pltpu.VMEM((2, chips, 3, width, depth), BF16),
            pltpu.VMEM((CHUNKS, size, 3 * width), F32),
            pltpu.VMEM((3, rows + HALO, width), F32),
            pltpu.VMEM((rows, width), BF16),
            pltpu.VMEM((rows, width), BF16),
            pltpu.VMEM((2, width, rows), BF16),
            pltpu.VMEM((2 * rows, rows), BF16),
            pltpu.VMEM((rows, 2 * rows), BF16),
            pltpu.VMEM((2, 2 * rows, width), F32),
            pltpu.VMEM((2, rows, width), F32),
            dma((chips, CHUNKS)),
            dma((chips, CHUNKS)),
            dma((chips, CHUNKS)),
            dma((chips, CHUNKS)),
            dma((CHUNKS,)),
            dma((2, chips)),
            dma((3,)),
            dma((CHUNKS + 2,)),
            dma((CHUNKS + 2,)),
        ],
        compiler_params=pltpu.CompilerParams(
            collective_id=0, has_side_effects=True, vmem_limit_bytes=48 * 1024 * 1024
        ),
        cost_estimate=pl.CostEstimate(
            flops=2 * rows * chips * 2 * depth * 3 * width,
            bytes_accessed=in_weight.size * 2,
            transcendentals=0,
        ),
    )(
        activations, in_weight, short_taps, long_filter, skip_gain[None, :],
        jnp.asarray(forward), jnp.asarray(inverse),
    )


def general(activations, in_weight, short_taps, long_filter, skip_gain):
    rows = activations.shape[0]
    channels = in_weight.shape[1]
    proj = jnp.einsum(
        "tk,sck->tsc",
        lax.all_gather(activations, "chan", axis=1, tiled=True),
        in_weight,
        preferred_element_type=F32,
    ).astype(BF16)
    earlier = from_behind(proj[rows - 2 :], "seq", 1)
    padded = jnp.concatenate([earlier, proj], axis=0).astype(F32)
    feat = (
        short_taps[:, 0, :] * padded[2:]
        + short_taps[:, 1, :] * padded[1:-1]
        + short_taps[:, 2, :] * padded[:-2]
    )
    gated = (feat[:, 1, :] * feat[:, 2, :]).astype(BF16)
    forward, inverse = (jnp.asarray(table) for table in half_tables(rows))
    seq_count = lax.axis_size("seq")
    all_lags = lax.all_gather(long_filter, "seq", axis=1, tiled=True)
    lag_blocks = all_lags.reshape(channels, seq_count, rows)
    spec = jnp.einsum("ft,cmt->mfc", forward, lag_blocks, preferred_element_type=F32)
    sign = (1.0 - 2.0 * (jnp.arange(2 * rows) % 2)).astype(F32)[:, None]
    spec = spec.at[1:].add(sign * spec[:-1])
    first = jnp.arange(rows)[:, None] == 0
    total = (jnp.zeros((rows, channels), F32), jnp.zeros((rows, channels), F32))
    moving = gated
    for section in range(seq_count):
        if section > 0:
            moving = from_behind(moving, "seq", 1)
        signal = jnp.dot(forward, moving, preferred_element_type=F32)
        part = times(
            spec[section, :rows], spec[section, rows:], signal[:rows], signal[rows:], first
        )
        total = (total[0] + part[0], total[1] + part[1])
    scale = jnp.where(first, 0.5, 1.0) / rows
    spectrum = jnp.concatenate([total[0] * scale, total[1] * scale], axis=0).astype(BF16)
    conv = jnp.dot(inverse, spectrum, preferred_element_type=F32)
    return (feat[:, 0, :] * (conv + skip_gain * gated.astype(F32))).astype(BF16)


def solution(mesh):
    in_specs = (
        P("seq", "chan"),
        P(None, "chan", None),
        P(None, None, "chan"),
        P("chan", "seq"),
        P("chan"),
    )
    out_specs = P("seq", "chan")
    chan = mesh.shape["chan"]
    if mesh.shape["seq"] == 2 and chan == 16:
        on_device = functools.partial(fused, chan // 2)
    else:
        on_device = general
    return jax.shard_map(
        on_device, mesh=mesh, in_specs=in_specs, out_specs=out_specs, check_vma=False
    )
```

time: 98.8 us -> 45.5 us (0.46)
  Pallas kernels: 0 us -> 38.4 us
  other arithmetic: 31.9 us -> 0 us
  waiting for transfers between devices: 23 us -> 0 us
  matrix products: 16.7 us -> 0 us
  between operations: 13.6 us -> 0.02 us
  blocking collectives: 8.72 us -> 0 us
  local copies, waits for them, and re-layouts: 1.47 us -> 6.44 us
  starting transfers between devices: 2.72 us -> 0 us
    pallas_call x0 -> x1, Pallas kernels: none -> 38.4 us  [fused(): pl.pallas_call(functools.partial(fused_kernel, chips), out_shape=jax.Shap...]
    convert_element_type x4 -> x0, other arithmetic: 31.4 us -> none  [the longest x1 15.7 us: tables(): jnp.sin(phase).astype(jnp.bfloat16)]
    dot_general x11 -> x0, matrix products: 16.7 us -> none  [the longest x1 7.51 us: on_device(): jnp.einsum('tk,sck->tsc', lax.all_gather(activations, 'chan', axis=1, til...]
    ppermute x2 -> x0, waiting for transfers between devices: 11.2 us -> none  [from_behind(): return lax.ppermute(block, axis, route)]
    all_gather x1 -> x0, waiting for transfers between devices: 11.1 us -> none  [on_device(): lax.all_gather(activations, 'chan', axis=1, tiled=True)]
    all_gather x1 -> x0, blocking collectives: 8.72 us -> none  [on_device(): all_lags = lax.all_gather(long_filter, 'seq', axis=1, tiled=True)]
    unnamed x15 -> x13, local copies, waits for them, and re-layouts: 1.24 us -> 6.44 us
    ppermute x2 -> x0, starting transfers between devices: 2.72 us -> none  [from_behind(): return lax.ppermute(block, axis, route)]
  transfers between devices with their start and end apart: 3 -> 0, of which waited for: 3 -> 0; matrix products, arithmetic and copies ran while one was open for 38% -> 0% of each run, Pallas kernels for 0% -> 0%
where the time goes in v1:
time: 45.5 us; the launch traced here: 44.8 us
  Pallas kernels  38.4 us (84%)
  local copies, waits for them, and re-layouts  6.44 us (14%)
    pallas_call x1, Pallas kernels, fused(): pl.pallas_call(functools.partial(fused_kernel, chips), out_shape=jax.Shap...  38.4 us
    unnamed x13, local copies, waits for them, and re-layouts  6.44 us

profile of v1, /device:TPU:2, one launch (start us, length us, event | category | flops | bytes accessed | tf_op | source)
XLA Modules:
  0.0 44.8 jit_solution(2566861689542456068)
XLA Ops:
  0.0 0.0 copy-start
  0.0 0.9 %copy-done = bf16[512,256]{1,0:T(8,128)(2,1)S(1)} copy-done((bf16[512,256]{1,0:T(8,128)(2,1)S(1)}, bf16[512,256]{1,0:T(8,128)(2,1)}, u32[]{:S(2)}) %copy-start) | copy-done | bytes 262168
  1.0 0.0 copy-start.1
  1.0 0.9 %copy-done.1 = bf16[256,512]{1,0:T(8,128)(2,1)S(1)} copy-done((bf16[256,512]{1,0:T(8,128)(2,1)S(1)}, bf16[256,512]{1,0:T(8,128)(2,1)}, u32[]{:S(2)}) %copy-start.1) | copy-done | bytes 262168
  1.9 0.0 copy-start.2
  1.9 0.7 %copy-done.2 = f32[3,3,256]{2,1,0:T(4,128)S(1)} copy-done((f32[3,3,256]{2,1,0:T(4,128)S(1)}, f32[3,3,256]{2,1,0:T(4,128)}, u32[]{:S(2)}) %copy-start.2) | copy-done | bytes 9240
  2.6 0.0 copy-start.3
  2.6 0.7 %copy-done.3 = f32[256]{0:T(256)S(1)} copy-done((f32[256]{0:T(256)S(1)}, f32[256]{0:T(256)}, u32[]{:S(2)}) %copy-start.3) | copy-done | bytes 1048
  3.3 0.0 copy-start.4
  3.3 1.2 %copy-done.4 = bf16[512,1024]{1,0:T(8,128)(2,1)S(1)} copy-done((bf16[512,1024]{1,0:T(8,128)(2,1)S(1)}, bf16[512,1024]{1,0:T(8,128)(2,1)}, u32[]{:S(2)}) %copy-start.4) | copy-done | bytes 1048600
  4.5 0.0 copy-start.5
  4.5 1.2 %copy-done.5 = bf16[1024,512]{1,0:T(8,128)(2,1)S(1)} copy-done((bf16[1024,512]{1,0:T(8,128)(2,1)S(1)}, bf16[1024,512]{1,0:T(8,128)(2,1)}, u32[]{:S(2)}) %copy-start.5) | copy-done | bytes 1048600
  5.7 38.4 %shard_map.73 = bf16[512,256]{1,0:T(8,128)(2,1)S(1)} custom-call(bf16[512,256]{1,0:T(8,128)(2,1)S(1)} %copy-done, bf16[3,256,4096]{2,1,0:T(8,128)(2,1)} %weight.1, f32[3,3,256]{2,1,0:T(4,128)S(1)} %copy-done.2, bf16[256,512]{1,0:T(8,128)(2,1)S(1)} %copy-done.1, f32[1,256]{1,0:T(1,128)S(1)} %bitcast.1, bf16[1024,512]{1,0:T(8,128)(2,1)S(1)} %copy-done.5, ...), custom_call_target="tpu_custom_call" | custom-call | flops 3221225472 | bytes 6291456 | tf_op jit(solution)/shard_map/pallas_call | solution.py:345
  44.1 0.7 %copy.9 = bf16[512,256]{1,0:T(8,128)(2,1)} copy(bf16[512,256]{1,0:T(8,128)(2,1)S(1)} %shard_map.73) | data formatting | bytes 524288
Async XLA Ops:
  0.0 0.9 %copy-start = (bf16[512,256]{1,0:T(8,128)(2,1)S(1)}, bf16[512,256]{1,0:T(8,128)(2,1)}, u32[]{:S(2)}) copy-start(bf16[512,256]{1,0:T(8,128)(2,1)} %act.1) | copy-start | bytes 786436
  1.0 0.9 %copy-start.1 = (bf16[256,512]{1,0:T(8,128)(2,1)S(1)}, bf16[256,512]{1,0:T(8,128)(2,1)}, u32[]{:S(2)}) copy-start(bf16[256,512]{1,0:T(8,128)(2,1)} %filt.1) | copy-start | bytes 786436
  1.9 0.7 %copy-start.2 = (f32[3,3,256]{2,1,0:T(4,128)S(1)}, f32[3,3,256]{2,1,0:T(4,128)}, u32[]{:S(2)}) copy-start(f32[3,3,256]{2,1,0:T(4,128)} %taps.1) | copy-start | bytes 27652
  2.6 0.7 %copy-start.3 = (f32[256]{0:T(256)S(1)}, f32[256]{0:T(256)}, u32[]{:S(2)}) copy-start(f32[256]{0:T(256)} %param.11) | copy-start | bytes 3076
  3.3 1.2 %copy-start.4 = (bf16[512,1024]{1,0:T(8,128)(2,1)S(1)}, bf16[512,1024]{1,0:T(8,128)(2,1)}, u32[]{:S(2)}) copy-start(bf16[512,1024]{1,0:T(8,128)(2,1)} %constant.5.clone.inv_in) | copy-start | bytes 3145732
  4.5 1.2 %copy-start.5 = (bf16[1024,512]{1,0:T(8,128)(2,1)S(1)}, bf16[1024,512]{1,0:T(8,128)(2,1)}, u32[]{:S(2)}) copy-start(bf16[1024,512]{1,0:T(8,128)(2,1)} %constant.4.clone.fwd_in) | copy-start | bytes 3145732

commit v2 on v1

--- a/solution.py
+++ b/solution.py
@@ -49,13 +49,13 @@
 
 
 def fused_kernel(
-    chips, act, weight, taps, filt, gain, fwd_in, inv_in, out,
-    blocks, wv, acc, proj, gated, gated_in, lags, fwd, inv, spec, total,
+    chips, act, weight, taps_in, filt, gain_in, fwd_in, inv_in, out,
+    blocks, wv, acc, proj, gated, gated_in, lags, fwd, inv, taps, gain, spec, total,
     ring_send, ring_recv, core_send, core_recv, own_sem, weight_sem, load_sem,
     seq_send, seq_recv,
 ):
     rows, depth = act.shape
-    width = taps.shape[-1]
+    width = taps_in.shape[-1]
     size = rows // CHUNKS
     far = chips // 2
     full = far - 1
@@ -137,6 +137,8 @@
     fwd_copy = pltpu.make_async_copy(fwd_in, fwd, load_sem.at[0])
     inv_copy = pltpu.make_async_copy(inv_in, inv, load_sem.at[1])
     lag_copy = pltpu.make_async_copy(filt, lags.at[seq], load_sem.at[2])
+    taps_copy = pltpu.make_async_copy(taps_in, taps, load_sem.at[3])
+    gain_copy = pltpu.make_async_copy(gain_in, gain, load_sem.at[4])
 
     for t in range(CHUNKS):
         own_copy(t).start()
@@ -146,6 +148,8 @@
     lag_copy.start()
     fwd_copy.start()
     inv_copy.start()
+    taps_copy.start()
+    gain_copy.start()
 
     barrier = pltpu.get_barrier_semaphore()
     for target in ((seq, ahead[0]), (seq, ahead[1]), (seq, sibling), (1 - seq, chan)):
@@ -167,17 +171,23 @@
     def gate(t):
         gated[chunk(t), :] = (short(1, t) * short(2, t)).astype(BF16)
 
-    def product(side, hop, t):
-        slots = slots_at(hop)
-
-        @pl.when(t == 0)
+    def product(hop, t):
+        parts = [(side, slot) for side in range(2) for slot in slots_at(hop)]
+
+        @pl.when(t == 1)
         def _():
-            for slot in slots:
+            for side, slot in parts:
                 weight_copy(side, slot).wait()
 
-        x = jnp.concatenate([blocks[side, slot, t] for slot in slots], axis=1)
+        x = jnp.concatenate(
+            [
+                blocks[side, slot, pl.ds(t - 1, 2)].reshape(2 * size, depth)
+                for side, slot in parts
+            ],
+            axis=1,
+        )
         w = jnp.concatenate(
-            [wv[side, slot].reshape(3 * width, depth) for slot in slots], axis=1
+            [wv[side, slot].reshape(3 * width, depth) for side, slot in parts], axis=1
         )
         return nt_dot(x, w)
 
@@ -213,26 +223,28 @@
         def _():
             filter_copy().start()
 
-        for side in range(2):
-            for hop in hops:
-                t = g - hop
-
-                @pl.when((t >= 0) & (t < CHUNKS))
-                def _(side=side, hop=hop, t=t):
-                    if side == 1:
-                        for slot in slots_at(hop):
-                            core_copy(slot, t).wait_recv()
-                    if side == 0 and hop == 0:
-                        own_copy(t).wait()
-                        acc[t] = product(side, hop, t)
-                    else:
-                        acc[t] += product(side, hop, t)
+        for hop in hops:
+            t = g - 1 - hop
+
+            @pl.when((t >= 0) & (t < CHUNKS) & (t % 2 == 1))
+            def _(hop=hop, t=t):
+                for slot in slots_at(hop):
+                    core_copy(slot, t - 1).wait_recv()
+                    core_copy(slot, t).wait_recv()
+                if hop == 0:
+                    own_copy(t - 1).wait()
+                    own_copy(t).wait()
+                    acc[t // 2] = product(hop, t)
+                else:
+                    acc[t // 2] += product(hop, t)
 
         @pl.when(g == full)
         def _():
             fwd_copy.wait()
             inv_copy.wait()
             lag_copy.wait()
+            taps_copy.wait()
+            gain_copy.wait()
 
             @pl.when(seq == 1)
             def _():
@@ -247,31 +259,34 @@
                 ).astype(F32)
                 spec[1] = nt_dot(fwd[...], lags[1]) + sign * spec[0]
 
-        done = g - far
-
-        @pl.when(done >= 0)
+        done = g - 1 - far
+
+        @pl.when((done >= 0) & (done % 2 == 1))
         def _():
             for stream in range(3):
                 cols = slice(stream * width, (stream + 1) * width)
-                proj[stream, pl.ds(pl.multiple_of(done * size + HALO, HALO), size), :] = (
-                    acc[done, :, cols].astype(BF16).astype(F32)
+                start = pl.multiple_of((done - 1) * size + HALO, HALO)
+                proj[stream, pl.ds(start, 2 * size), :] = (
+                    acc[done // 2, :, cols].astype(BF16).astype(F32)
                 )
 
             @pl.when((seq == 0) & (done == CHUNKS - 1))
             def _():
                 halo_copy().start()
 
-            @pl.when((seq == 0) | (done > 0))
-            def _():
-                gate(done)
-
-            @pl.when(seq == 0)
-            def _():
-                gated_copy(done).start()
+            for t in (done - 1, done):
+
+                @pl.when((seq == 0) | (t > 0))
+                def _(t=t):
+                    gate(t)
+
+                @pl.when(seq == 0)
+                def _(t=t):
+                    gated_copy(t).start()
 
         return carry
 
-    lax.fori_loop(0, CHUNKS + far, step, 0)
+    lax.fori_loop(0, CHUNKS + far + 1, step, 0)
 
     @pl.when(seq == 1)
     def _():
@@ -340,23 +355,25 @@
     forward, inverse = half_tables(rows)
     size = rows // CHUNKS
     here = pl.BlockSpec(memory_space=pltpu.VMEM)
-    there = pl.BlockSpec(memory_space=pl.ANY)
+    there = pl.BlockSpec(memory_space=pltpu.HBM)
     dma = pltpu.SemaphoreType.DMA
     return pl.pallas_call(
         functools.partial(fused_kernel, chips),
         out_shape=jax.ShapeDtypeStruct((rows, width), BF16),
-        in_specs=[there, there, here, there, here, there, there],
+        in_specs=[there] * 7,
         out_specs=here,
         scratch_shapes=[
             pltpu.VMEM((2, chips, CHUNKS, size, depth), BF16),
             pltpu.VMEM((2, chips, 3, width, depth), BF16),
-            pltpu.VMEM((CHUNKS, size, 3 * width), F32),
+            pltpu.VMEM((CHUNKS // 2, 2 * size, 3 * width), F32),
             pltpu.VMEM((3, rows + HALO, width), F32),
             pltpu.VMEM((rows, width), BF16),
             pltpu.VMEM((rows, width), BF16),
             pltpu.VMEM((2, width, rows), BF16),
             pltpu.VMEM((2 * rows, rows), BF16),
             pltpu.VMEM((rows, 2 * rows), BF16),
+            pltpu.VMEM((3, 3, width), F32),
+            pltpu.VMEM((1, width), F32),
             pltpu.VMEM((2, 2 * rows, width), F32),
             pltpu.VMEM((2, rows, width), F32),
             dma((chips, CHUNKS)),
@@ -365,12 +382,12 @@
             dma((chips, CHUNKS)),
             dma((CHUNKS,)),
             dma((2, chips)),
-            dma((3,)),
+            dma((5,)),
             dma((CHUNKS + 2,)),
             dma((CHUNKS + 2,)),
         ],
         compiler_params=pltpu.CompilerParams(
-            collective_id=0, has_side_effects=True, vmem_limit_bytes=48 * 1024 * 1024
+            collective_id=0, has_side_effects=True, vmem_limit_bytes=63 * 1024 * 1024
         ),
         cost_estimate=pl.CostEstimate(
             flops=2 * rows * chips * 2 * depth * 3 * width,

time: 45.5 us -> 43.8 us (0.963); the launches traced: 44.8 us -> 43.7 us
  local copies, waits for them, and re-layouts: 6.44 us -> 1.67 us
  Pallas kernels: 38.4 us -> 42 us
    unnamed x13 -> x1, local copies, waits for them, and re-layouts: 6.44 us -> 1.67 us
    pallas_call x1, Pallas kernels: 38.4 us -> 42 us  [fused(): pl.pallas_call(functools.partial(fused_kernel, chips), out_shape=jax.Shap...]
where the time goes in v2:
time: 43.8 us; the launch traced here: 43.7 us
  Pallas kernels  42 us (96%)
  local copies, waits for them, and re-layouts  1.67 us (4%)
    pallas_call x1, Pallas kernels, fused(): pl.pallas_call(functools.partial(fused_kernel, chips), out_shape=jax.Shap...  42 us
    unnamed x1, local copies, waits for them, and re-layouts  1.67 us

profile of v2, /device:TPU:2, one launch (start us, length us, event | category | flops | bytes accessed | tf_op | source)
XLA Modules:
  0.0 43.7 jit_solution(2551830247938577974)
XLA Ops:
  0.0 42.0 %shard_map.73 = bf16[512,256]{1,0:T(8,128)(2,1)} custom-call(bf16[512,256]{1,0:T(8,128)(2,1)} %act.1, bf16[3,256,4096]{2,1,0:T(8,128)(2,1)} %weight.1, f32[3,3,256]{2,1,0:T(4,128)} %taps_in.1, bf16[256,512]{1,0:T(8,128)(2,1)} %filt.1, f32[1,256]{1,0:T(1,128)} %bitcast.1, bf16[1024,512]{1,0:T(8,128)(2,1)} %constant.4.clone.fwd_in, ...), custom_call_target="tpu_custom_call" | custom-call | flops 3221225472 | bytes 6291456 | tf_op jit(solution)/shard_map/pallas_call | solution.py:360
  42.0 1.7 %copy.9 = bf16[512,256]{1,0:T(8,128)(2,1)} copy(bf16[512,256]{1,0:T(8,128)(2,1)} %shard_map.73) | data formatting | bytes 524288

commit v3 on v2

--- a/solution.py
+++ b/solution.py
@@ -189,7 +189,7 @@
         w = jnp.concatenate(
             [wv[side, slot].reshape(3 * width, depth) for side, slot in parts], axis=1
         )
-        return nt_dot(x, w)
+        return nt_dot(w, x)
 
     hops = list(range(far, -1, -1))
 
@@ -267,7 +267,7 @@
                 cols = slice(stream * width, (stream + 1) * width)
                 start = pl.multiple_of((done - 1) * size + HALO, HALO)
                 proj[stream, pl.ds(start, 2 * size), :] = (
-                    acc[done // 2, :, cols].astype(BF16).astype(F32)
+                    acc[done // 2, cols, :].astype(BF16).T.astype(F32)
                 )
 
             @pl.when((seq == 0) & (done == CHUNKS - 1))
@@ -365,7 +365,7 @@
         scratch_shapes=[
             pltpu.VMEM((2, chips, CHUNKS, size, depth), BF16),
             pltpu.VMEM((2, chips, 3, width, depth), BF16),
-            pltpu.VMEM((CHUNKS // 2, 2 * size, 3 * width), F32),
+            pltpu.VMEM((CHUNKS // 2, 3 * width, 2 * size), F32),
             pltpu.VMEM((3, rows + HALO, width), F32),
             pltpu.VMEM((rows, width), BF16),
             pltpu.VMEM((rows, width), BF16),

time: 43.8 us -> 43.9 us (level)
  no operation moved by 1% of the time
where the time goes in v3:
time: 43.9 us; the launch traced here: 43.8 us
  Pallas kernels  42.1 us (96%)
  local copies, waits for them, and re-layouts  1.67 us (4%)
    pallas_call x1, Pallas kernels, fused(): pl.pallas_call(functools.partial(fused_kernel, chips), out_shape=jax.Shap...  42.1 us
    unnamed x1, local copies, waits for them, and re-layouts  1.67 us

profile of v3, /device:TPU:2, one launch (start us, length us, event | category | flops | bytes accessed | tf_op | source)
XLA Modules:
  0.0 43.8 jit_solution(11510167233526221441)
XLA Ops:
  0.0 42.1 %shard_map.73 = bf16[512,256]{1,0:T(8,128)(2,1)} custom-call(bf16[512,256]{1,0:T(8,128)(2,1)} %act.1, bf16[3,256,4096]{2,1,0:T(8,128)(2,1)} %weight.1, f32[3,3,256]{2,1,0:T(4,128)} %taps_in.1, bf16[256,512]{1,0:T(8,128)(2,1)} %filt.1, f32[1,256]{1,0:T(1,128)} %bitcast.1, bf16[1024,512]{1,0:T(8,128)(2,1)} %constant.4.clone.fwd_in, ...), custom_call_target="tpu_custom_call" | custom-call | flops 3221225472 | bytes 6291456 | tf_op jit(solution)/shard_map/pallas_call | solution.py:360
  42.1 1.7 %copy.9 = bf16[512,256]{1,0:T(8,128)(2,1)} copy(bf16[512,256]{1,0:T(8,128)(2,1)} %shard_map.73) | data formatting | bytes 524288

commit v4 on v3

--- a/solution.py
+++ b/solution.py
@@ -191,102 +191,103 @@
         )
         return nt_dot(w, x)
 
-    hops = list(range(far, -1, -1))
-
-    def step(g, carry):
-        for hop in hops:
-            t = g - hop
-
-            @pl.when((t >= 0) & (t < CHUNKS))
-            def _(hop=hop, t=t):
-                if hop == 0:
-                    for d in range(2):
-                        ring_copy(d, 1, t).start()
-                    core_copy(0, t).start()
-                elif hop < far:
-                    for d in range(2):
-                        ring_copy(d, hop, t).wait_recv()
-                        if hop < full:
-                            ring_copy(d, hop + 1, t).start()
-                        else:
-
-                            @pl.when(t % 2 == d)
-                            def _(d=d):
-                                ring_copy(d, far, t).start()
-
-                        core_copy(slot_of(d, hop), t).start()
+    def pass_on(hop, t):
+        for d in range(2):
+            if hop < far:
+                ring_copy(d, hop, t).wait_recv()
+                if hop < full:
+                    ring_copy(d, hop + 1, t).start()
                 else:
-                    ring_copy(0, far, t).wait_recv()
-                    core_copy(last_slot, t).start()
-
-        @pl.when((g == 0) & (seq == 0))
+
+                    @pl.when(t % 2 == d)
+                    def _(d=d):
+                        ring_copy(d, far, t).start()
+
+        if hop == far:
+            ring_copy(0, far, t).wait_recv()
+        for slot in slots_at(hop):
+            core_copy(slot, t).start()
+
+    def project(hop, t):
+        for slot in slots_at(hop):
+            core_copy(slot, t - 1).wait_recv()
+            core_copy(slot, t).wait_recv()
+        if hop == 0:
+            own_copy(t - 1).wait()
+            own_copy(t).wait()
+            acc[t // 2] = product(hop, t)
+        else:
+            acc[t // 2] += product(hop, t)
+
+    def finalize(done):
+        for stream in range(3):
+            cols = slice(stream * width, (stream + 1) * width)
+            start = pl.multiple_of((done - 1) * size + HALO, HALO)
+            proj[stream, pl.ds(start, 2 * size), :] = (
+                acc[done // 2, cols, :].astype(BF16).T.astype(F32)
+            )
+
+        @pl.when((seq == 0) & (done == CHUNKS - 1))
         def _():
-            filter_copy().start()
-
-        for hop in hops:
-            t = g - 1 - hop
-
-            @pl.when((t >= 0) & (t < CHUNKS) & (t % 2 == 1))
-            def _(hop=hop, t=t):
-                for slot in slots_at(hop):
-                    core_copy(slot, t - 1).wait_recv()
-                    core_copy(slot, t).wait_recv()
-                if hop == 0:
-                    own_copy(t - 1).wait()
-                    own_copy(t).wait()
-                    acc[t // 2] = product(hop, t)
-                else:
-                    acc[t // 2] += product(hop, t)
-
-        @pl.when(g == full)
+            halo_copy().start()
+
+        for t in (done - 1, done):
+
+            @pl.when((seq == 0) | (t > 0))
+            def _(t=t):
+                gate(t)
+
+            @pl.when(seq == 0)
+            def _(t=t):
+                gated_copy(t).start()
+
+    def filter_spectra():
+        fwd_copy.wait()
+        inv_copy.wait()
+        lag_copy.wait()
+        taps_copy.wait()
+        gain_copy.wait()
+
+        @pl.when(seq == 1)
         def _():
-            fwd_copy.wait()
-            inv_copy.wait()
-            lag_copy.wait()
-            taps_copy.wait()
-            gain_copy.wait()
-
-            @pl.when(seq == 1)
-            def _():
-                filter_copy().wait_recv()
-
-            spec[0] = nt_dot(fwd[...], lags[0])
-
-            @pl.when(seq == 1)
-            def _():
-                sign = 1.0 - 2.0 * (
-                    lax.broadcasted_iota(jnp.int32, (2 * rows, width), 0) % 2
-                ).astype(F32)
-                spec[1] = nt_dot(fwd[...], lags[1]) + sign * spec[0]
-
-        done = g - 1 - far
-
-        @pl.when((done >= 0) & (done % 2 == 1))
+            filter_copy().wait_recv()
+
+        spec[0] = nt_dot(fwd[...], lags[0])
+
+        @pl.when(seq == 1)
         def _():
-            for stream in range(3):
-                cols = slice(stream * width, (stream + 1) * width)
-                start = pl.multiple_of((done - 1) * size + HALO, HALO)
-                proj[stream, pl.ds(start, 2 * size), :] = (
-                    acc[done // 2, cols, :].astype(BF16).T.astype(F32)
-                )
-
-            @pl.when((seq == 0) & (done == CHUNKS - 1))
-            def _():
-                halo_copy().start()
-
-            for t in (done - 1, done):
-
-                @pl.when((seq == 0) | (t > 0))
-                def _(t=t):
-                    gate(t)
-
-                @pl.when(seq == 0)
-                def _(t=t):
-                    gated_copy(t).start()
-
+            sign = 1.0 - 2.0 * (
+                lax.broadcasted_iota(jnp.int32, (2 * rows, width), 0) % 2
+            ).astype(F32)
+            spec[1] = nt_dot(fwd[...], lags[1]) + sign * spec[0]
+
+    def send_own(t, carry):
+        for d in range(2):
+            ring_copy(d, 1, t).start()
+        core_copy(0, t).start()
         return carry
 
-    lax.fori_loop(0, CHUNKS + far + 1, step, 0)
+    lax.fori_loop(0, CHUNKS, send_own, 0)
+
+    @pl.when(seq == 0)
+    def _():
+        filter_copy().start()
+
+    for hop in range(1, far + 1):
+
+        def pair(p, carry, hop=hop):
+            t = 2 * p + 1
+            pass_on(hop, t - 1)
+            pass_on(hop, t)
+            project(hop - 1, t)
+            if hop == far:
+                project(far, t)
+                finalize(t)
+            return carry
+
+        lax.fori_loop(0, CHUNKS // 2, pair, 0)
+        if hop == 2:
+            filter_spectra()
 
     @pl.when(seq == 1)
     def _():

time: 43.9 us -> 38.1 us (0.87)
  Pallas kernels: 42.1 us -> 36.3 us
    pallas_call x1, Pallas kernels: 42.1 us -> 36.3 us  [fused(): pl.pallas_call(functools.partial(fused_kernel, chips), out_shape=jax.Shap...]
where the time goes in v4:
time: 38.1 us; the launch traced here: 38 us
  Pallas kernels  36.3 us (95%)
  local copies, waits for them, and re-layouts  1.67 us (4%)
    pallas_call x1, Pallas kernels, fused(): pl.pallas_call(functools.partial(fused_kernel, chips), out_shape=jax.Shap...  36.3 us
    unnamed x1, local copies, waits for them, and re-layouts  1.67 us

profile of v4, /device:TPU:2, one launch (start us, length us, event | category | flops | bytes accessed | tf_op | source)
XLA Modules:
  0.0 38.0 jit_solution(10637239757123490464)
XLA Ops:
  0.0 36.3 %shard_map.73 = bf16[512,256]{1,0:T(8,128)(2,1)} custom-call(bf16[512,256]{1,0:T(8,128)(2,1)} %act.1, bf16[3,256,4096]{2,1,0:T(8,128)(2,1)} %weight.1, f32[3,3,256]{2,1,0:T(4,128)} %taps_in.1, bf16[256,512]{1,0:T(8,128)(2,1)} %filt.1, f32[1,256]{1,0:T(1,128)} %bitcast.1, bf16[1024,512]{1,0:T(8,128)(2,1)} %constant.4.clone.fwd_in, ...), custom_call_target="tpu_custom_call" | custom-call | flops 3221225472 | bytes 6291456 | tf_op jit(solution)/shard_map/pallas_call | solution.py:361
  36.3 1.7 %copy.9 = bf16[512,256]{1,0:T(8,128)(2,1)} copy(bf16[512,256]{1,0:T(8,128)(2,1)} %shard_map.73) | data formatting | bytes 524288

commit v5 on v4

--- a/solution.py
+++ b/solution.py
@@ -85,7 +85,7 @@
         return pl.ds(pl.multiple_of(t * size, size), size)
 
     def ring_copy(d, hop, t):
-        src = act.at[chunk(t)] if hop == 1 else blocks.at[0, slot_of(d, hop - 1), t]
+        src = blocks.at[0, slot_of(d, hop - 1), t]
         slot = slot_of(d, hop)
         return pltpu.make_async_remote_copy(
             src_ref=src, dst_ref=blocks.at[0, slot, t],
@@ -94,7 +94,7 @@
         )
 
     def core_copy(slot, t):
-        src = act.at[chunk(t)] if slot == 0 else blocks.at[0, slot, t]
+        src = blocks.at[0, slot, t]
         return pltpu.make_async_remote_copy(
             src_ref=src, dst_ref=blocks.at[1, slot, t],
             send_sem=core_send.at[slot, t], recv_sem=core_recv.at[slot, t],
@@ -142,15 +142,6 @@
 
     for t in range(CHUNKS):
         own_copy(t).start()
-    for slot in range(last_slot + 1):
-        for side in range(2):
-            weight_copy(side, slot).start()
-    lag_copy.start()
-    fwd_copy.start()
-    inv_copy.start()
-    taps_copy.start()
-    gain_copy.start()
-
     barrier = pltpu.get_barrier_semaphore()
     for target in ((seq, ahead[0]), (seq, ahead[1]), (seq, sibling), (1 - seq, chan)):
         pl.semaphore_signal(barrier, inc=1, device_id=target, device_id_type=MESH)
@@ -213,8 +204,6 @@
             core_copy(slot, t - 1).wait_recv()
             core_copy(slot, t).wait_recv()
         if hop == 0:
-            own_copy(t - 1).wait()
-            own_copy(t).wait()
             acc[t // 2] = product(hop, t)
         else:
             acc[t // 2] += product(hop, t)
@@ -262,12 +251,23 @@
             spec[1] = nt_dot(fwd[...], lags[1]) + sign * spec[0]
 
     def send_own(t, carry):
+        own_copy(t).wait()
         for d in range(2):
             ring_copy(d, 1, t).start()
         core_copy(0, t).start()
         return carry
 
     lax.fori_loop(0, CHUNKS, send_own, 0)
+
+    for hop in range(far + 1):
+        for slot in slots_at(hop):
+            for side in range(2):
+                weight_copy(side, slot).start()
+    lag_copy.start()
+    fwd_copy.start()
+    inv_copy.start()
+    taps_copy.start()
+    gain_copy.start()
 
     @pl.when(seq == 0)
     def _():
@@ -289,6 +289,23 @@
         if hop == 2:
             filter_spectra()
 
+    def finish(t, carry):
+        for hop in range(1, far):
+            for d in range(2):
+                ring_copy(d, hop, t).wait_send()
+        for d in range(2):
+
+            @pl.when(t % 2 == d)
+            def _(d=d):
+                ring_copy(d, far, t).wait_send()
+
+        for slot in range(last_slot + 1):
+            core_copy(slot, t).wait_send()
+
+        return carry
+
+    lax.fori_loop(0, CHUNKS, finish, 0)
+
     @pl.when(seq == 1)
     def _():
         halo_copy().wait_recv()
@@ -323,29 +340,10 @@
             short(0, t) * (conv[here] + gain[...] * gated[here, :].astype(F32))
         ).astype(BF16)
 
-    def finish(t, carry):
-        for hop in range(1, far):
-            for d in range(2):
-                ring_copy(d, hop, t).wait_send()
-        for d in range(2):
-
-            @pl.when(t % 2 == d)
-            def _(d=d):
-                ring_copy(d, far, t).wait_send()
-
-        for slot in range(last_slot + 1):
-            core_copy(slot, t).wait_send()
-
-        @pl.when(seq == 0)
-        def _():
-            gated_copy(t).wait_send()
-
-        return carry
-
-    lax.fori_loop(0, CHUNKS, finish, 0)
-
     @pl.when(seq == 0)
     def _():
+        for t in range(CHUNKS):
+            gated_copy(t).wait_send()
         halo_copy().wait_send()
         filter_copy().wait_send()
 
@@ -360,7 +358,7 @@
     dma = pltpu.SemaphoreType.DMA
     return pl.pallas_call(
         functools.partial(fused_kernel, chips),
-        out_shape=jax.ShapeDtypeStruct((rows, width), BF16),
+        out_shape=pltpu.VMEM((rows, width), BF16),
         in_specs=[there] * 7,
         out_specs=here,
         scratch_shapes=[

time: 38.1 us -> 36.1 us (0.948)
  Pallas kernels: 36.3 us -> 35.2 us
  local copies, waits for them, and re-layouts: 1.67 us -> 0.71 us
    pallas_call x1, Pallas kernels: 36.3 us -> 35.2 us  [fused(): pl.pallas_call(functools.partial(fused_kernel, chips), out_shape=pltpu.VM...]
    unnamed x1, local copies, waits for them, and re-layouts: 1.67 us -> 0.71 us
where the time goes in v5:
time: 36.1 us; the launch traced here: 35.9 us
  Pallas kernels  35.2 us (98%)
  local copies, waits for them, and re-layouts  0.71 us (2%)
    pallas_call x1, Pallas kernels, fused(): pl.pallas_call(functools.partial(fused_kernel, chips), out_shape=pltpu.VM...  35.2 us

profile of v5, /device:TPU:2, one launch (start us, length us, event | category | flops | bytes accessed | tf_op | source)
XLA Modules:
  0.0 35.9 jit_solution(18214773052039982026)
XLA Ops:
  0.0 35.2 %shard_map.73 = bf16[512,256]{1,0:T(8,128)(2,1)S(1)} custom-call(bf16[512,256]{1,0:T(8,128)(2,1)} %act.1, bf16[3,256,4096]{2,1,0:T(8,128)(2,1)} %weight.1, f32[3,3,256]{2,1,0:T(4,128)} %taps_in.1, bf16[256,512]{1,0:T(8,128)(2,1)} %filt.1, f32[1,256]{1,0:T(1,128)} %bitcast.1, bf16[1024,512]{1,0:T(8,128)(2,1)} %constant.4.clone.fwd_in, ...), custom_call_target="tpu_custom_call" | custom-call | flops 3221225472 | bytes 6291456 | tf_op jit(solution)/shard_map/pallas_call | solution.py:359
  35.2 0.7 %copy.9 = bf16[512,256]{1,0:T(8,128)(2,1)} copy(bf16[512,256]{1,0:T(8,128)(2,1)S(1)} %shard_map.73) | data formatting | bytes 524288

commit v6 on v5

--- a/solution.py
+++ b/solution.py
@@ -182,22 +182,37 @@
         )
         return nt_dot(w, x)
 
+    def send(d, hop, t):
+        if hop == far:
+
+            @pl.when(t % 2 == d)
+            def _():
+                ring_copy(d, full, CHUNKS - 2 + t // 2).wait_send()
+                ring_copy(d, far, t).start()
+
+        else:
+
+            @pl.when(t >= 2)
+            def _():
+                ring_copy(d, hop, t - 2).wait_send()
+
+            if hop > 1:
+
+                @pl.when(t < 2)
+                def _():
+                    ring_copy(d, hop - 1, t + CHUNKS - 2).wait_send()
+
+            ring_copy(d, hop, t).start()
+
     def pass_on(hop, t):
-        for d in range(2):
-            if hop < far:
-                ring_copy(d, hop, t).wait_recv()
-                if hop < full:
-                    ring_copy(d, hop + 1, t).start()
-                else:
-
-                    @pl.when(t % 2 == d)
-                    def _(d=d):
-                        ring_copy(d, far, t).start()
-
         if hop == far:
             ring_copy(0, far, t).wait_recv()
-        for slot in slots_at(hop):
-            core_copy(slot, t).start()
+            core_copy(last_slot, t).start()
+        else:
+            for d in range(2):
+                ring_copy(d, hop, t).wait_recv()
+                core_copy(slot_of(d, hop), t).start()
+                send(d, hop + 1, t)
 
     def project(hop, t):
         for slot in slots_at(hop):
@@ -252,12 +267,12 @@
 
     def send_own(t, carry):
         own_copy(t).wait()
+        core_copy(0, t).start()
         for d in range(2):
-            ring_copy(d, 1, t).start()
-        core_copy(0, t).start()
+            send(d, 1, t)
         return carry
 
-    lax.fori_loop(0, CHUNKS, send_own, 0)
+    lax.fori_loop(0, 2, send_own, 0)
 
     for hop in range(far + 1):
         for slot in slots_at(hop):
@@ -273,6 +288,8 @@
     def _():
         filter_copy().start()
 
+    lax.fori_loop(2, CHUNKS, send_own, 0)
+
     for hop in range(1, far + 1):
 
         def pair(p, carry, hop=hop):
@@ -290,9 +307,6 @@
             filter_spectra()
 
     def finish(t, carry):
-        for hop in range(1, far):
-            for d in range(2):
-                ring_copy(d, hop, t).wait_send()
         for d in range(2):
 
             @pl.when(t % 2 == d)

time: 36.1 us -> 36 us (level)
  no operation moved by 1% of the time
where the time goes in v6:
time: 36 us; the launch traced here: 35.9 us
  Pallas kernels  35.2 us (98%)
  local copies, waits for them, and re-layouts  0.71 us (2%)
    pallas_call x1, Pallas kernels, fused(): pl.pallas_call(functools.partial(fused_kernel, chips), out_shape=pltpu.VM...  35.2 us

profile of v6, /device:TPU:2, one launch (start us, length us, event | category | flops | bytes accessed | tf_op | source)
XLA Modules:
  0.0 35.9 jit_solution(16520634592767499583)
XLA Ops:
  0.0 35.2 %shard_map.73 = bf16[512,256]{1,0:T(8,128)(2,1)S(1)} custom-call(bf16[512,256]{1,0:T(8,128)(2,1)} %act.1, bf16[3,256,4096]{2,1,0:T(8,128)(2,1)} %weight.1, f32[3,3,256]{2,1,0:T(4,128)} %taps_in.1, bf16[256,512]{1,0:T(8,128)(2,1)} %filt.1, f32[1,256]{1,0:T(1,128)} %bitcast.1, bf16[1024,512]{1,0:T(8,128)(2,1)} %constant.4.clone.fwd_in, ...), custom_call_target="tpu_custom_call" | custom-call | flops 3221225472 | bytes 6291456 | tf_op jit(solution)/shard_map/pallas_call | solution.py:373
  35.2 0.7 %copy.9 = bf16[512,256]{1,0:T(8,128)(2,1)} copy(bf16[512,256]{1,0:T(8,128)(2,1)S(1)} %shard_map.73) | data formatting | bytes 524288

commit v7 on v5

--- a/solution.py
+++ b/solution.py
@@ -15,6 +15,7 @@
 BF16 = jnp.bfloat16
 CHUNKS = 4
 HALO = 8
+Q, KV, QKV = slice(0, 1), slice(1, 3), slice(0, 3)
 
 
 def from_behind(block, axis, distance):
@@ -50,7 +51,7 @@
 
 def fused_kernel(
     chips, act, weight, taps_in, filt, gain_in, fwd_in, inv_in, out,
-    blocks, wv, acc, proj, gated, gated_in, lags, fwd, inv, taps, gain, spec, total,
+    blocks, wv, acc, proj, gated, gated_in, lags, fwd, inv, taps, gain, spec, total, early,
     ring_send, ring_recv, core_send, core_recv, own_sem, weight_sem, load_sem,
     seq_send, seq_recv,
 ):
@@ -110,11 +111,14 @@
     def gated_copy(t):
         return seq_copy(gated.at[chunk(t)], gated_in.at[chunk(t)], t)
 
-    def halo_copy():
-        return seq_copy(proj.at[:, pl.ds(rows, HALO)], proj.at[:, pl.ds(0, HALO)], CHUNKS)
+    def halo_copy(streams):
+        return seq_copy(
+            proj.at[streams, pl.ds(rows, HALO)], proj.at[streams, pl.ds(0, HALO)],
+            CHUNKS + (streams is Q),
+        )
 
     def filter_copy():
-        return seq_copy(filt, lags.at[0], CHUNKS + 1)
+        return seq_copy(filt, lags.at[0], CHUNKS + 2)
 
     def own_copy(t):
         return pltpu.make_async_copy(act.at[chunk(t)], blocks.at[0, 0, t], own_sem.at[t])
@@ -162,73 +166,76 @@
     def gate(t):
         gated[chunk(t), :] = (short(1, t) * short(2, t)).astype(BF16)
 
-    def product(hop, t):
+    def arrive(hop, d, t):
+        ring_copy(d, hop, t).wait_recv()
+        core_copy(slot_of(d, hop), t).start()
+
+    def pass_on(hop, index):
+        for d in range(2):
+            t = index ^ d
+            arrive(hop, d, t)
+            if hop < full or index % 2 == 0:
+                ring_copy(d, hop + 1, t).start()
+
+    def arrive_far(p):
+        for d in range(2):
+            arrive(far, d, 2 * p + d)
+
+    def project(hop, p, streams=QKV):
         parts = [(side, slot) for side in range(2) for slot in slots_at(hop)]
-
-        @pl.when(t == 1)
-        def _():
+        if streams is not Q:
             for side, slot in parts:
-                weight_copy(side, slot).wait()
-
+                if p == 0:
+                    weight_copy(side, slot).wait()
+                if side == 1:
+                    core_copy(slot, 2 * p).wait_recv()
+                    core_copy(slot, 2 * p + 1).wait_recv()
         x = jnp.concatenate(
             [
-                blocks[side, slot, pl.ds(t - 1, 2)].reshape(2 * size, depth)
+                blocks[side, slot, pl.ds(2 * p, 2)].reshape(2 * size, depth)
                 for side, slot in parts
             ],
             axis=1,
         )
+        count = streams.stop - streams.start
         w = jnp.concatenate(
-            [wv[side, slot].reshape(3 * width, depth) for side, slot in parts], axis=1
-        )
-        return nt_dot(w, x)
-
-    def pass_on(hop, t):
-        for d in range(2):
-            if hop < far:
-                ring_copy(d, hop, t).wait_recv()
-                if hop < full:
-                    ring_copy(d, hop + 1, t).start()
-                else:
-
-                    @pl.when(t % 2 == d)
-                    def _(d=d):
-                        ring_copy(d, far, t).start()
-
-        if hop == far:
-            ring_copy(0, far, t).wait_recv()
-        for slot in slots_at(hop):
-            core_copy(slot, t).start()
-
-    def project(hop, t):
-        for slot in slots_at(hop):
-            core_copy(slot, t - 1).wait_recv()
-            core_copy(slot, t).wait_recv()
+            [wv[side, slot, streams].reshape(count * width, depth) for side, slot in parts],
+            axis=1,
+        )
+        here = slice(streams.start * width, streams.stop * width)
         if hop == 0:
-            acc[t // 2] = product(hop, t)
+            acc[p, here] = nt_dot(w, x)
         else:
-            acc[t // 2] += product(hop, t)
-
-    def finalize(done):
-        for stream in range(3):
+            acc[p, here] += nt_dot(w, x)
+
+    def round_up(p, streams):
+        for stream in range(streams.start, streams.stop):
             cols = slice(stream * width, (stream + 1) * width)
-            start = pl.multiple_of((done - 1) * size + HALO, HALO)
-            proj[stream, pl.ds(start, 2 * size), :] = (
-                acc[done // 2, cols, :].astype(BF16).T.astype(F32)
+            proj[stream, pl.ds(2 * p * size + HALO, 2 * size), :] = (
+                acc[p, cols, :].astype(BF16).T.astype(F32)
             )
 
-        @pl.when((seq == 0) & (done == CHUNKS - 1))
-        def _():
-            halo_copy().start()
-
-        for t in (done - 1, done):
-
-            @pl.when((seq == 0) | (t > 0))
-            def _(t=t):
+        if p == CHUNKS // 2 - 1:
+
+            @pl.when(seq == 0)
+            def _():
+                halo_copy(streams).start()
+
+    def gate_pair(p):
+        for t in (2 * p, 2 * p + 1):
+            if t > 0:
                 gate(t)
 
-            @pl.when(seq == 0)
-            def _(t=t):
-                gated_copy(t).start()
+                @pl.when(seq == 0)
+                def _(t=t):
+                    gated_copy(t).start()
+
+            else:
+
+                @pl.when(seq == 0)
+                def _(t=t):
+                    gate(t)
+                    gated_copy(t).start()
 
     def filter_spectra():
         fwd_copy.wait()
@@ -250,15 +257,17 @@
             ).astype(F32)
             spec[1] = nt_dot(fwd[...], lags[1]) + sign * spec[0]
 
-    def send_own(t, carry):
-        own_copy(t).wait()
-        for d in range(2):
-            ring_copy(d, 1, t).start()
-        core_copy(0, t).start()
-        return carry
-
-    lax.fori_loop(0, CHUNKS, send_own, 0)
-
+    def send_own(p):
+        for t in (2 * p, 2 * p + 1):
+            own_copy(t).wait()
+        for index in (2 * p, 2 * p + 1):
+            for d in range(2):
+                ring_copy(d, 1, index ^ d).start()
+        for t in (2 * p, 2 * p + 1):
+            core_copy(0, t).start()
+
+    send_own(0)
+    send_own(1)
     for hop in range(far + 1):
         for slot in slots_at(hop):
             for side in range(2):
@@ -273,21 +282,37 @@
     def _():
         filter_copy().start()
 
-    for hop in range(1, far + 1):
-
-        def pair(p, carry, hop=hop):
-            t = 2 * p + 1
-            pass_on(hop, t - 1)
-            pass_on(hop, t)
-            project(hop - 1, t)
-            if hop == far:
-                project(far, t)
-                finalize(t)
-            return carry
-
-        lax.fori_loop(0, CHUNKS // 2, pair, 0)
-        if hop == 2:
-            filter_spectra()
+    pass_on(1, 0)
+    pass_on(1, 1)
+    project(0, 0)
+    pass_on(1, 2)
+    project(0, 1)
+    pass_on(2, 0)
+    pass_on(2, 1)
+    project(1, 0)
+    pass_on(1, 3)
+    pass_on(3, 0)
+    pass_on(3, 1)
+    project(2, 0)
+    pass_on(2, 2)
+    project(1, 1)
+    filter_spectra()
+    pass_on(2, 3)
+    project(3, 0)
+    arrive_far(0)
+    project(2, 1)
+    pass_on(3, 2)
+    project(4, 0)
+    round_up(0, QKV)
+    gate_pair(0)
+    pass_on(3, 3)
+    project(3, 1)
+    arrive_far(1)
+    project(4, 1, KV)
+    round_up(1, KV)
+    gate_pair(1)
+    project(4, 1, Q)
+    round_up(1, Q)
 
     def finish(t, carry):
         for hop in range(1, far):
@@ -308,24 +333,33 @@
 
     @pl.when(seq == 1)
     def _():
-        halo_copy().wait_recv()
+        halo_copy(KV).wait_recv()
         gate(0)
 
     first = lax.broadcasted_iota(jnp.int32, (rows, width), 0) == 0
 
-    def term(lag, source):
-        signal = jnp.dot(fwd[...], source[...], preferred_element_type=F32)
+    def term(lag, signal):
         return times(
             spec[lag, :rows], spec[lag, rows:], signal[:rows], signal[rows:], first
         )
 
-    total[0], total[1] = term(0, gated)
+    total[0], total[1] = term(
+        0, jnp.dot(fwd[...], gated[...], preferred_element_type=F32)
+    )
 
     @pl.when(seq == 1)
     def _():
-        for t in range(CHUNKS):
+        half = rows // 2
+        for t in range(CHUNKS // 2):
             gated_copy(t).wait_recv()
-        real_part, imag_part = term(1, gated_in)
+        early[...] = jnp.dot(
+            fwd[:, :half], gated_in[:half], preferred_element_type=F32
+        )
+        for t in range(CHUNKS // 2, CHUNKS):
+            gated_copy(t).wait_recv()
+        late = jnp.dot(fwd[:, half:], gated_in[half:], preferred_element_type=F32)
+        real_part, imag_part = term(1, early[...] + late)
+        halo_copy(Q).wait_recv()
         total[0] += real_part
         total[1] += imag_part
 
@@ -344,7 +378,8 @@
     def _():
         for t in range(CHUNKS):
             gated_copy(t).wait_send()
-        halo_copy().wait_send()
+        halo_copy(KV).wait_send()
+        halo_copy(Q).wait_send()
         filter_copy().wait_send()
 
 
@@ -375,6 +410,7 @@
             pltpu.VMEM((1, width), F32),
             pltpu.VMEM((2, 2 * rows, width), F32),
             pltpu.VMEM((2, rows, width), F32),
+            pltpu.VMEM((2 * rows, width), F32),
             dma((chips, CHUNKS)),
             dma((chips, CHUNKS)),
             dma((chips, CHUNKS)),
@@ -382,8 +418,8 @@
             dma((CHUNKS,)),
             dma((2, chips)),
             dma((5,)),
-            dma((CHUNKS + 2,)),
-            dma((CHUNKS + 2,)),
+            dma((CHUNKS + 3,)),
+            dma((CHUNKS + 3,)),
         ],
         compiler_params=pltpu.CompilerParams(
             collective_id=0, has_side_effects=True, vmem_limit_bytes=63 * 1024 * 1024

time: 36.1 us -> 36.2 us (level)
  no operation moved by 1% of the time
where the time goes in v7:
time: 36.2 us; the launch traced here: 36 us
  Pallas kernels  35.2 us (97%)
  local copies, waits for them, and re-layouts  0.71 us (2%)
    pallas_call x1, Pallas kernels, fused(): pl.pallas_call(functools.partial(fused_kernel, chips), out_shape=pltpu.VM...  35.2 us

profile of v7, /device:TPU:2, one launch (start us, length us, event | category | flops | bytes accessed | tf_op | source)
XLA Modules:
  0.0 36.0 jit_solution(5063727227089690307)
XLA Ops:
  0.0 35.2 %shard_map.73 = bf16[512,256]{1,0:T(8,128)(2,1)S(1)} custom-call(bf16[512,256]{1,0:T(8,128)(2,1)} %act.1, bf16[3,256,4096]{2,1,0:T(8,128)(2,1)} %weight.1, f32[3,3,256]{2,1,0:T(4,128)} %taps_in.1, bf16[256,512]{1,0:T(8,128)(2,1)} %filt.1, f32[1,256]{1,0:T(1,128)} %bitcast.1, bf16[1024,512]{1,0:T(8,128)(2,1)} %constant.4.clone.fwd_in, ...), custom_call_target="tpu_custom_call" | custom-call | flops 3221225472 | bytes 6291456 | tf_op jit(solution)/shard_map/pallas_call | solution.py:394
  35.3 0.7 %copy.9 = bf16[512,256]{1,0:T(8,128)(2,1)} copy(bf16[512,256]{1,0:T(8,128)(2,1)S(1)} %shard_map.73) | data formatting | bytes 524288

commit v8 on v5

--- a/solution.py
+++ b/solution.py
@@ -13,7 +13,7 @@
 MESH = pl.DeviceIdType.MESH
 F32 = jnp.float32
 BF16 = jnp.bfloat16
-CHUNKS = 4
+CHUNKS = 2
 HALO = 8
 
 

time: 36.1 us -> 37.5 us (1.039)
  Pallas kernels: 35.2 us -> 36.6 us
    pallas_call x1, Pallas kernels: 35.2 us -> 36.6 us  [fused(): pl.pallas_call(functools.partial(fused_kernel, chips), out_shape=pltpu.VM...]
where the time goes in v8:
time: 37.5 us; the launch traced here: 37.3 us
  Pallas kernels  36.6 us (98%)
  local copies, waits for them, and re-layouts  0.71 us (2%)
    pallas_call x1, Pallas kernels, fused(): pl.pallas_call(functools.partial(fused_kernel, chips), out_shape=pltpu.VM...  36.6 us

profile of v8, /device:TPU:2, one launch (start us, length us, event | category | flops | bytes accessed | tf_op | source)
XLA Modules:
  0.0 37.3 jit_solution(18331024872388774629)
XLA Ops:
  0.0 36.6 %shard_map.73 = bf16[512,256]{1,0:T(8,128)(2,1)S(1)} custom-call(bf16[512,256]{1,0:T(8,128)(2,1)} %act.1, bf16[3,256,4096]{2,1,0:T(8,128)(2,1)} %weight.1, f32[3,3,256]{2,1,0:T(4,128)} %taps_in.1, bf16[256,512]{1,0:T(8,128)(2,1)} %filt.1, f32[1,256]{1,0:T(1,128)} %bitcast.1, bf16[1024,512]{1,0:T(8,128)(2,1)} %constant.4.clone.fwd_in, ...), custom_call_target="tpu_custom_call" | custom-call | flops 3221225472 | bytes 6291456 | tf_op jit(solution)/shard_map/pallas_call | solution.py:359
  36.6 0.7 %copy.9 = bf16[512,256]{1,0:T(8,128)(2,1)} copy(bf16[512,256]{1,0:T(8,128)(2,1)S(1)} %shard_map.73) | data formatting | bytes 524288

commit v9 on v5

--- a/solution.py
+++ b/solution.py
@@ -50,7 +50,7 @@
 
 def fused_kernel(
     chips, act, weight, taps_in, filt, gain_in, fwd_in, inv_in, out,
-    blocks, wv, acc, proj, gated, gated_in, lags, fwd, inv, taps, gain, spec, total,
+    blocks, wv, acc, proj, gated, lags, fwd, inv, taps, gain, spec, total,
     ring_send, ring_recv, core_send, core_recv, own_sem, weight_sem, load_sem,
     seq_send, seq_recv,
 ):
@@ -74,9 +74,11 @@
     sibling = chip * 2 + 1 - core
 
     def slot_of(d, hop):
-        if hop == 0:
-            return 0
-        return last_slot if hop == far else 1 + d * full + hop - 1
+        if isinstance(hop, int):
+            if hop == 0:
+                return 0
+            return last_slot if hop == far else d * full + hop
+        return jnp.where(hop == 0, 0, jnp.where(hop == far, last_slot, d * full + hop))
 
     def slots_at(hop):
         return [slot_of(0, hop)] if hop in (0, far) else [slot_of(0, hop), slot_of(1, hop)]
@@ -108,7 +110,7 @@
         )
 
     def gated_copy(t):
-        return seq_copy(gated.at[chunk(t)], gated_in.at[chunk(t)], t)
+        return seq_copy(gated.at[0, chunk(t)], gated.at[1, chunk(t)], t)
 
     def halo_copy():
         return seq_copy(proj.at[:, pl.ds(rows, HALO)], proj.at[:, pl.ds(0, HALO)], CHUNKS)
@@ -160,53 +162,48 @@
         )
 
     def gate(t):
-        gated[chunk(t), :] = (short(1, t) * short(2, t)).astype(BF16)
-
-    def product(hop, t):
-        parts = [(side, slot) for side in range(2) for slot in slots_at(hop)]
-
-        @pl.when(t == 1)
-        def _():
-            for side, slot in parts:
-                weight_copy(side, slot).wait()
-
-        x = jnp.concatenate(
-            [
-                blocks[side, slot, pl.ds(t - 1, 2)].reshape(2 * size, depth)
-                for side, slot in parts
-            ],
-            axis=1,
-        )
-        w = jnp.concatenate(
-            [wv[side, slot].reshape(3 * width, depth) for side, slot in parts], axis=1
-        )
-        return nt_dot(w, x)
+        gated[0, chunk(t), :] = (short(1, t) * short(2, t)).astype(BF16)
 
     def pass_on(hop, t):
         for d in range(2):
-            if hop < far:
+
+            @pl.when(hop < far)
+            def _(d=d):
                 ring_copy(d, hop, t).wait_recv()
-                if hop < full:
-                    ring_copy(d, hop + 1, t).start()
-                else:
-
-                    @pl.when(t % 2 == d)
-                    def _(d=d):
-                        ring_copy(d, far, t).start()
-
-        if hop == far:
-            ring_copy(0, far, t).wait_recv()
-        for slot in slots_at(hop):
-            core_copy(slot, t).start()
-
-    def project(hop, t):
-        for slot in slots_at(hop):
-            core_copy(slot, t - 1).wait_recv()
-            core_copy(slot, t).wait_recv()
-        if hop == 0:
-            acc[t // 2] = product(hop, t)
-        else:
-            acc[t // 2] += product(hop, t)
+
+            @pl.when((hop < full) | ((hop == full) & (t % 2 == d)))
+            def _(d=d):
+                ring_copy(d, hop + 1, t).start()
+
+            @pl.when((hop < far) | (d == 0))
+            def _(d=d):
+                if d == 0:
+
+                    @pl.when(hop == far)
+                    def _():
+                        ring_copy(0, far, t).wait_recv()
+
+                core_copy(slot_of(d, hop), t).start()
+
+    def project(slot, p):
+        @pl.when(p == 0)
+        def _():
+            for side in range(2):
+                pltpu.make_async_copy(
+                    weight.at[:, :, pl.ds(0, depth)], wv.at[side, slot],
+                    weight_sem.at[side, slot],
+                ).wait()
+
+        core_copy(slot, 2 * p).wait_recv()
+        core_copy(slot, 2 * p + 1).wait_recv()
+        x = jnp.concatenate(
+            [blocks[side, slot, pl.ds(2 * p, 2)].reshape(2 * size, depth) for side in range(2)],
+            axis=1,
+        )
+        w = jnp.concatenate(
+            [wv[side, slot].reshape(3 * width, depth) for side in range(2)], axis=1
+        )
+        acc[p] += nt_dot(w, x)
 
     def finalize(done):
         for stream in range(3):
@@ -241,14 +238,18 @@
         def _():
             filter_copy().wait_recv()
 
-        spec[0] = nt_dot(fwd[...], lags[0])
+        def transform(m, carry):
+            spec[m] = nt_dot(fwd[...], lags[m])
+            return carry
+
+        lax.fori_loop(0, 1 + seq, transform, 0)
 
         @pl.when(seq == 1)
         def _():
             sign = 1.0 - 2.0 * (
                 lax.broadcasted_iota(jnp.int32, (2 * rows, width), 0) % 2
             ).astype(F32)
-            spec[1] = nt_dot(fwd[...], lags[1]) + sign * spec[0]
+            spec[1] += sign * spec[0]
 
     def send_own(t, carry):
         own_copy(t).wait()
@@ -273,21 +274,30 @@
     def _():
         filter_copy().start()
 
-    for hop in range(1, far + 1):
-
-        def pair(p, carry, hop=hop):
-            t = 2 * p + 1
-            pass_on(hop, t - 1)
-            pass_on(hop, t)
-            project(hop - 1, t)
-            if hop == far:
-                project(far, t)
-                finalize(t)
+    acc[...] = jnp.zeros_like(acc)
+
+    def stage(n, carry):
+        hop, p = 1 + n // 2, n % 2
+        pass_on(hop, 2 * p)
+        pass_on(hop, 2 * p + 1)
+
+        def one(j, carry):
+            project(jnp.minimum(hop - 1 + j * full, last_slot), p)
             return carry
 
-        lax.fori_loop(0, CHUNKS // 2, pair, 0)
-        if hop == 2:
+        lax.fori_loop(0, 1 + (hop > 1).astype(jnp.int32) + (hop == far).astype(jnp.int32), one, 0)
+
+        @pl.when(n == 4)
+        def _():
             filter_spectra()
+
+        @pl.when(hop == far)
+        def _():
+            finalize(2 * p + 1)
+
+        return carry
+
+    lax.fori_loop(0, 2 * far, stage, 0)
 
     def finish(t, carry):
         for hop in range(1, far):
@@ -313,21 +323,23 @@
 
     first = lax.broadcasted_iota(jnp.int32, (rows, width), 0) == 0
 
-    def term(lag, source):
-        signal = jnp.dot(fwd[...], source[...], preferred_element_type=F32)
-        return times(
+    total[...] = jnp.zeros_like(total)
+
+    def term(lag, carry):
+        @pl.when(lag == 1)
+        def _():
+            for t in range(CHUNKS):
+                gated_copy(t).wait_recv()
+
+        signal = jnp.dot(fwd[...], gated[lag], preferred_element_type=F32)
+        real_part, imag_part = times(
             spec[lag, :rows], spec[lag, rows:], signal[:rows], signal[rows:], first
         )
-
-    total[0], total[1] = term(0, gated)
-
-    @pl.when(seq == 1)
-    def _():
-        for t in range(CHUNKS):
-            gated_copy(t).wait_recv()
-        real_part, imag_part = term(1, gated_in)
         total[0] += real_part
         total[1] += imag_part
+        return carry
+
+    lax.fori_loop(0, 1 + seq, term, 0)
 
     scale = jnp.where(first, 0.5, 1.0) / rows
     spectrum = jnp.concatenate(
@@ -337,7 +349,7 @@
     for t in range(CHUNKS):
         here = slice(t * size, (t + 1) * size)
         out[here, :] = (
-            short(0, t) * (conv[here] + gain[...] * gated[here, :].astype(F32))
+            short(0, t) * (conv[here] + gain[...] * gated[0, here, :].astype(F32))
         ).astype(BF16)
 
     @pl.when(seq == 0)
@@ -366,8 +378,7 @@
             pltpu.VMEM((2, chips, 3, width, depth), BF16),
             pltpu.VMEM((CHUNKS // 2, 3 * width, 2 * size), F32),
             pltpu.VMEM((3, rows + HALO, width), F32),
-            pltpu.VMEM((rows, width), BF16),
-            pltpu.VMEM((rows, width), BF16),
+            pltpu.VMEM((2, rows, width), BF16),
             pltpu.VMEM((2, width, rows), BF16),
             pltpu.VMEM((2 * rows, rows), BF16),
             pltpu.VMEM((rows, 2 * rows), BF16),

time: 36.1 us -> 36.1 us (level)
  no operation moved by 1% of the time
where the time goes in v9:
time: 36.1 us; the launch traced here: 35.9 us
  Pallas kernels  35.2 us (98%)
  local copies, waits for them, and re-layouts  0.71 us (2%)
    pallas_call x1, Pallas kernels, fused(): pl.pallas_call(functools.partial(fused_kernel, chips), out_shape=pltpu.VM...  35.2 us

profile of v9, /device:TPU:2, one launch (start us, length us, event | category | flops | bytes accessed | tf_op | source)
XLA Modules:
  0.0 35.9 jit_solution(10226838559125120120)
XLA Ops:
  0.0 35.2 %shard_map.73 = bf16[512,256]{1,0:T(8,128)(2,1)S(1)} custom-call(bf16[512,256]{1,0:T(8,128)(2,1)} %act.1, bf16[3,256,4096]{2,1,0:T(8,128)(2,1)} %weight.1, f32[3,3,256]{2,1,0:T(4,128)} %taps_in.1, bf16[256,512]{1,0:T(8,128)(2,1)} %filt.1, f32[1,256]{1,0:T(1,128)} %bitcast.1, bf16[1024,512]{1,0:T(8,128)(2,1)} %constant.4.clone.fwd_in, ...), custom_call_target="tpu_custom_call" | custom-call | flops 3221225472 | bytes 6291456 | tf_op jit(solution)/shard_map/pallas_call | solution.py:371
  35.2 0.7 %copy.9 = bf16[512,256]{1,0:T(8,128)(2,1)} copy(bf16[512,256]{1,0:T(8,128)(2,1)S(1)} %shard_map.73) | data formatting | bytes 524288

commit v10 on v9

--- a/solution.py
+++ b/solution.py
@@ -80,9 +80,6 @@
             return last_slot if hop == far else d * full + hop
         return jnp.where(hop == 0, 0, jnp.where(hop == far, last_slot, d * full + hop))
 
-    def slots_at(hop):
-        return [slot_of(0, hop)] if hop in (0, far) else [slot_of(0, hop), slot_of(1, hop)]
-
     def chunk(t):
         return pl.ds(pl.multiple_of(t * size, size), size)
 
@@ -121,20 +118,16 @@
     def own_copy(t):
         return pltpu.make_async_copy(act.at[chunk(t)], blocks.at[0, 0, t], own_sem.at[t])
 
-    def weight_copy(side, slot):
-        if slot == 0:
-            origin = chip
-        elif slot == last_slot:
-            origin = chip_at(place + far)
-        elif slot <= full:
-            origin = chip_at(place - slot)
-        else:
-            origin = chip_at(place + slot - full)
-        block = origin * 2 + (core if side == 0 else 1 - core)
-        cols = pl.ds(pl.multiple_of(block * depth, depth), depth)
-        return pltpu.make_async_copy(
-            weight.at[:, :, cols], wv.at[side, slot], weight_sem.at[side, slot]
-        )
+    def load_weights(hop, ways=2):
+        for d in range(ways):
+            slot = slot_of(d, hop)
+            origin = chip_at(place - hop if d == 0 else place + hop)
+            for side in range(2):
+                block = origin * 2 + (core if side == 0 else 1 - core)
+                cols = pl.ds(pl.multiple_of(block * depth, depth), depth)
+                pltpu.make_async_copy(
+                    weight.at[:, :, cols], wv.at[side, slot], weight_sem.at[side, slot]
+                ).start()
 
     fwd_copy = pltpu.make_async_copy(fwd_in, fwd, load_sem.at[0])
     inv_copy = pltpu.make_async_copy(inv_in, inv, load_sem.at[1])
@@ -260,15 +253,8 @@
 
     lax.fori_loop(0, CHUNKS, send_own, 0)
 
-    for hop in range(far + 1):
-        for slot in slots_at(hop):
-            for side in range(2):
-                weight_copy(side, slot).start()
-    lag_copy.start()
-    fwd_copy.start()
-    inv_copy.start()
-    taps_copy.start()
-    gain_copy.start()
+    load_weights(0, 1)
+    load_weights(1)
 
     @pl.when(seq == 0)
     def _():
@@ -278,10 +264,26 @@
 
     def stage(n, carry):
         hop, p = 1 + n // 2, n % 2
-        pass_on(hop, 2 * p)
-        pass_on(hop, 2 * p + 1)
+
+        @pl.when((p == 0) & (hop < full))
+        def _():
+            load_weights(hop + 1)
+
+        @pl.when((p == 0) & (hop == full))
+        def _():
+            load_weights(far, 1)
+
+        @pl.when(n == 1)
+        def _():
+            for load in (lag_copy, fwd_copy, inv_copy, taps_copy, gain_copy):
+                load.start()
 
         def one(j, carry):
+            @pl.when((j == 2) | ((j == 0) & (hop < far)))
+            def _():
+                pass_on(hop, 2 * p)
+                pass_on(hop, 2 * p + 1)
+
             project(jnp.minimum(hop - 1 + j * full, last_slot), p)
             return carry
 

time: 36.1 us -> 35.7 us (0.989)
  Pallas kernels: 35.2 us -> 34.8 us
    pallas_call x1, Pallas kernels: 35.2 us -> 34.8 us  [fused(): pl.pallas_call(functools.partial(fused_kernel, chips), out_shape=pltpu.VM...]
where the time goes in v10:
time: 35.7 us; the launch traced here: 35.5 us
  Pallas kernels  34.8 us (97%)
  local copies, waits for them, and re-layouts  0.71 us (2%)
    pallas_call x1, Pallas kernels, fused(): pl.pallas_call(functools.partial(fused_kernel, chips), out_shape=pltpu.VM...  34.8 us

profile of v10, /device:TPU:2, one launch (start us, length us, event | category | flops | bytes accessed | tf_op | source)
XLA Modules:
  0.0 35.5 jit_solution(18141084008464212418)
XLA Ops:
  0.0 34.8 %shard_map.73 = bf16[512,256]{1,0:T(8,128)(2,1)S(1)} custom-call(bf16[512,256]{1,0:T(8,128)(2,1)} %act.1, bf16[3,256,4096]{2,1,0:T(8,128)(2,1)} %weight.1, f32[3,3,256]{2,1,0:T(4,128)} %taps_in.1, bf16[256,512]{1,0:T(8,128)(2,1)} %filt.1, f32[1,256]{1,0:T(1,128)} %bitcast.1, bf16[1024,512]{1,0:T(8,128)(2,1)} %constant.4.clone.fwd_in, ...), custom_call_target="tpu_custom_call" | custom-call | flops 3221225472 | bytes 6291456 | tf_op jit(solution)/shard_map/pallas_call | solution.py:373
  34.8 0.7 %copy.9 = bf16[512,256]{1,0:T(8,128)(2,1)} copy(bf16[512,256]{1,0:T(8,128)(2,1)S(1)} %shard_map.73) | data formatting | bytes 524288

commit v11 on v10

--- a/solution.py
+++ b/solution.py
@@ -256,10 +256,6 @@
     load_weights(0, 1)
     load_weights(1)
 
-    @pl.when(seq == 0)
-    def _():
-        filter_copy().start()
-
     acc[...] = jnp.zeros_like(acc)
 
     def stage(n, carry):
@@ -277,6 +273,10 @@
         def _():
             for load in (lag_copy, fwd_copy, inv_copy, taps_copy, gain_copy):
                 load.start()
+
+            @pl.when(seq == 0)
+            def _():
+                filter_copy().start()
 
         def one(j, carry):
             @pl.when((j == 2) | ((j == 0) & (hop < far)))

time: 35.7 us -> 35.7 us (level)
  no operation moved by 1% of the time
where the time goes in v11:
time: 35.7 us; the launch traced here: 35.5 us
  Pallas kernels  34.8 us (97%)
  local copies, waits for them, and re-layouts  0.71 us (2%)
    pallas_call x1, Pallas kernels, fused(): pl.pallas_call(functools.partial(fused_kernel, chips), out_shape=pltpu.VM...  34.8 us

profile of v11, /device:TPU:2, one launch (start us, length us, event | category | flops | bytes accessed | tf_op | source)
XLA Modules:
  0.0 35.5 jit_solution(12599299516595066501)
XLA Ops:
  0.0 34.8 %shard_map.73 = bf16[512,256]{1,0:T(8,128)(2,1)S(1)} custom-call(bf16[512,256]{1,0:T(8,128)(2,1)} %act.1, bf16[3,256,4096]{2,1,0:T(8,128)(2,1)} %weight.1, f32[3,3,256]{2,1,0:T(4,128)} %taps_in.1, bf16[256,512]{1,0:T(8,128)(2,1)} %filt.1, f32[1,256]{1,0:T(1,128)} %bitcast.1, bf16[1024,512]{1,0:T(8,128)(2,1)} %constant.4.clone.fwd_in, ...), custom_call_target="tpu_custom_call" | custom-call | flops 3221225472 | bytes 6291456 | tf_op jit(solution)/shard_map/pallas_call | solution.py:373
  34.8 0.7 %copy.9 = bf16[512,256]{1,0:T(8,128)(2,1)} copy(bf16[512,256]{1,0:T(8,128)(2,1)S(1)} %shard_map.73) | data formatting | bytes 524288
